TPU v7x, 512 devices: a whole 4x4x16 slice. The times are simulated.
512 devices in a mesh: phase: 4 (over x), expert: 32 (over z_hi, y, core), tensor: 4 (over z_lo).
Axes of the slice: x: 4, y: 4, z: 16 (z_hi: 4, z_lo: 4; z = z_hi * 4 + z_lo), core: 2. Of those that a mesh axis runs over, the one named last changes fastest.
Arguments:
- forward_routes: int32 [4, 2048, 6], P('phase', 'expert'), may hold values from 0 to 95, all different within a row; in each aligned block of 64 rows (0 to 63, 64 to 127, ..., all dimensions but the last counted through in order) at most 6 rows name the same one
- forward_gates: float32 [4, 2048, 6], P('phase', 'expert'), may hold values from 0.05 to 1
- hidden_rows: bfloat16 [4, 96, 32, 6, 1024], P('phase', 'expert', None, None, 'tensor'), may hold values from -6 to 6
- down_weight: bfloat16 [4, 96, 1024, 2560], P('phase', 'expert', 'tensor'), may hold values from -0.1875 to 0.1875
- shared_hidden: bfloat16 [4, 2048, 1536], P('phase', 'expert', 'tensor'), may hold values from -6 to 6
- shared_weight: bfloat16 [4, 1536, 2560], P('phase', 'tensor', 'expert'), may hold values from -0.15625 to 0.15625
- backward_routes: int32 [4, 2048, 6], P('phase', 'expert'), may hold values from 0 to 95, all different within a row; in each aligned block of 64 rows (0 to 63, 64 to 127, ..., all dimensions but the last counted through in order) at most 6 rows name the same one
- backward_gates: float32 [4, 2048, 6], P('phase', 'expert'), may hold values from 0.05 to 1
- cotangent: bfloat16 [4, 2048, 2560], P('phase', 'expert', 'tensor'), may hold values from -6 to 6
Outputs:
- forward_next: bfloat16 [4, 2048, 2560], P('phase', 'expert', 'tensor')
- hidden_grad: bfloat16 [4, 96, 32, 6, 1024], P('phase', 'expert', None, None, 'tensor')
- shared_grad: bfloat16 [4, 2048, 1536], P('phase', 'expert', 'tensor')
Inputs may be any that keep to these rules, and one draw needn't show every extreme that they name: `forward_routes`: each token names 6 different experts. The tokens of one token group (the 64 rows of one device) name any one expert 6 times at most, and some group reaches that. `backward_routes`: as for forward_routes.
All inputs are finite; a program needn't handle non-finite values.
Results may differ from a plain program's by a relative error of at most 0.0049.
Values may be sent and summed in bfloat16 or wider, within the bound.
No kernel may reach another device: no remote copies, remote signals or barrier semaphores. Data moves between devices by JAX's collectives and lax.ppermute only.
A program may use at most 64 MiB of HBM per device.

v0:
```python
import jax
import jax.numpy as jnp
from jax import lax
from jax.sharding import PartitionSpec as P


def in_blocks(array, dim, length):
    before, after = (array.shape[:dim], array.shape[dim + 1 :])
    return jnp.moveaxis(array.reshape(*before, length, -1, *after), dim, 0)


def summed_on_arrival(array, axis, dim):
    parts = in_blocks(array, dim, lax.axis_size(axis))
    arrived = lax.all_to_all(parts, axis, split_axis=0, concat_axis=0, tiled=True)
    return arrived.sum(axis=0)


def shifted(value, axis, steps):
    count = lax.axis_size(axis)
    pairs = [(source, (source + steps) % count) for source in range(count)]
    return lax.ppermute(value, axis, pairs)


def sent_to_all(array, axis):
    length = lax.axis_size(axis)
    return lax.all_to_all(
        jnp.broadcast_to(array[None], (length, *array.shape)), axis, 0, 0, tiled=True
    )


def joined_along(parts, dim):
    parts = jnp.moveaxis(parts, 0, dim)
    dims = parts.shape
    return parts.reshape(*dims[:dim], dims[dim] * dims[dim + 1], *dims[dim + 2 :])


def gathered_copies(array, axis, dim):
    parts = sent_to_all(array, axis)
    return joined_along(parts, dim)


def slot_numbers(routes, experts):
    numbers = jnp.arange(experts, dtype=jnp.int32)
    onehot = (routes[:, :, None] == numbers[None, None, :]).astype(jnp.int32)
    per_token = jnp.sum(onehot, axis=1)
    before = jnp.cumsum(per_token, axis=0) - per_token
    return jnp.sum(onehot * before[:, None, :], axis=2)


def row_positions(routes, experts_here, groups, capacity):
    slot_index = slot_numbers(routes, experts_here * groups)
    holder = routes // experts_here
    within = routes - holder * experts_here
    return ((within * groups + holder) * capacity + slot_index).reshape(-1)


def place_rows(gates, values, positions, total_rows):
    scaled = (gates[:, :, None] * values[:, None, :].astype(jnp.float32)).astype(jnp.bfloat16)
    outgoing = jnp.zeros((total_rows, values.shape[1]), jnp.bfloat16)
    return outgoing.at[positions].set(scaled.reshape(-1, values.shape[1]))


def on_device(
    forward_routes,
    forward_gates,
    hidden_rows,
    down_weight,
    shared_hidden,
    shared_weight,
    backward_routes,
    backward_gates,
    cotangent,
):
    experts_here = down_weight.shape[1]
    features = down_weight.shape[3]
    capacity = hidden_rows.shape[3]
    groups = lax.axis_size("expert")
    token_count = forward_routes.shape[1]
    top_count = forward_routes.shape[2]
    hidden = hidden_rows[0]
    weight = down_weight[0]
    local_shared = shared_hidden[0]
    shared_piece = shared_weight[0]
    shared_part = jnp.dot(
        local_shared,
        lax.all_gather(shared_piece, "expert", axis=1, tiled=True),
        preferred_element_type=jnp.float32,
    )
    fore_positions = row_positions(forward_routes[0], experts_here, groups, capacity)
    fore_gates = forward_gates[0]
    partial_value = jnp.einsum(
        "egmh,ehd->egmd", hidden, weight, preferred_element_type=jnp.float32
    ).astype(jnp.bfloat16)
    arrived = lax.all_to_all(partial_value, "expert", split_axis=1, concat_axis=1, tiled=True)
    picked = arrived.reshape(-1, features)[fore_positions].reshape(token_count, top_count, features)
    summand = shared_part + jnp.sum(picked.astype(jnp.float32) * fore_gates[:, :, None], axis=1)
    summed = summed_on_arrival(summand, "tensor", 1)
    layer_out = summed.astype(jnp.bfloat16)
    handed = shifted(layer_out, "phase", 1)
    cotangent_whole = gathered_copies(cotangent[0], "tensor", 1)
    back_positions = row_positions(backward_routes[0], experts_here, groups, capacity)
    total_rows = experts_here * groups * capacity
    local_cot = cotangent[0]
    outgoing = place_rows(backward_gates[0], local_cot, back_positions, total_rows)
    received_part = lax.all_to_all(
        outgoing.reshape(experts_here, groups, capacity, local_cot.shape[1]),
        "expert",
        split_axis=1,
        concat_axis=1,
        tiled=True,
    )
    received = lax.all_gather(received_part, "tensor", axis=3, tiled=True)
    hidden_back = jnp.einsum(
        "egmd,ehd->egmh", received, weight, preferred_element_type=jnp.float32
    ).astype(jnp.bfloat16)
    shared_back = lax.dot_general(
        cotangent_whole,
        lax.all_gather(shared_piece, "expert", axis=1, tiled=True),
        (((1,), (1,)), ((), ())),
        preferred_element_type=jnp.float32,
    )
    return (handed[None], hidden_back[None], shared_back.astype(jnp.bfloat16)[None])


def solution(mesh):
    return jax.shard_map(
        on_device,
        mesh=mesh,
        in_specs=(
            P("phase", "expert", None),
            P("phase", "expert", None),
            P("phase", "expert", None, None, "tensor"),
            P("phase", "expert", "tensor", None),
            P("phase", "expert", "tensor"),
            P("phase", "tensor", "expert"),
            P("phase", "expert", None),
            P("phase", "expert", None),
            P("phase", "expert", "tensor"),
        ),
        out_specs=(
            P("phase", "expert", "tensor"),
            P("phase", "expert", None, None, "tensor"),
            P("phase", "expert", "tensor"),
        ),
        check_vma=False,
    )
```

profile of v0, /device:TPU:1, one launch (start us, length us, event | category | flops | bytes accessed | tf_op | source)
XLA Modules:
  0.0 387.4 jit_solution(6066048009045506084)
XLA Ops:
  9.6 0.9 bitcast_convert_fusion
  11.0 2.4 scatter_custom_fusion
  13.7 1.0 copy.44
  14.7 19.4 %all-to-all-start.2 = ((bf16[3,32,6,640]{3,2,0,1:T(8,128)(2,1)}), bf16[3,32,6,640]{3,2,0,1:T(8,128)(2,1)S(1)}, u32[]{:S(2)}, u32[]{:S(2)}) async-start(bf16[3,32,6,640]{3,2,0,1:T(8,128)(2,1)} %copy.44), calls=%async_computation.2 | async-start | bytes 1966080 | tf_op jit(solution)/shard_map/all_to_all | solution.py:105
  34.1 3.1 convolution_convert_fusion
  37.2 3.5 copy.35
  40.7 42.7 %all-to-all-done.2 = bf16[3,32,6,640]{3,2,0,1:T(8,128)(2,1)S(1)} async-done(((bf16[3,32,6,640]{3,2,0,1:T(8,128)(2,1)}), bf16[3,32,6,640]{3,2,0,1:T(8,128)(2,1)S(1)}, u32[]{:S(2)}, u32[]{:S(2)}) %all-to-all-start.2) | async-done | bytes 737312 | tf_op jit(solution)/shard_map/all_to_all | solution.py:105
  83.5 8.6 %all-to-all-start = ((bf16[3,32,6,2560]{3,2,0,1:T(8,128)(2,1)}), bf16[3,32,6,2560]{3,2,0,1:T(8,128)(2,1)}, u32[]{:S(2)}, u32[]{:S(2)}) async-start(bf16[3,32,6,2560]{3,2,0,1:T(8,128)(2,1)} %copy.35), calls=%async_computation | async-start | bytes 7864320 | tf_op jit(solution)/shard_map/all_to_all | solution.py:94
  92.9 1.0 copy.45
  94.0 180.4 %all-to-all-done = bf16[3,32,6,2560]{3,2,0,1:T(8,128)(2,1)} async-done(((bf16[3,32,6,2560]{3,2,0,1:T(8,128)(2,1)}), bf16[3,32,6,2560]{3,2,0,1:T(8,128)(2,1)}, u32[]{:S(2)}, u32[]{:S(2)}) %all-to-all-start) | async-done | bytes 2949152 | tf_op jit(solution)/shard_map/all_to_all | solution.py:94
  275.1 8.2 %all-to-all-start.3 = ((bf16[4,64,640]{2,1,0:T(8,128)(2,1)}), bf16[4,64,640]{2,1,0:T(8,128)(2,1)}, u32[]{:S(2)}, u32[]{:S(2)}) async-start(bf16[4,64,640]{2,1,0:T(8,128)(2,1)} %broadcast_in_dim.26), calls=%async_computation.3 | async-start | bytes 655360 | tf_op jit(solution)/shard_map/all_to_all | solution.py:26
  284.4 4.4 %copy.36 = bf16[3,32,6,2560]{3,2,1,0:T(8,128)(2,1)} copy(bf16[3,32,6,2560]{3,2,0,1:T(8,128)(2,1)} %all-to-all-done) | data formatting | bytes 5898240 | tf_op jit(solution)/shard_map/all_to_all | solution.py:94
  288.8 4.1 %reshape.226 = bf16[576,2560]{1,0:T(8,128)(2,1)S(1)} reshape(bf16[3,32,6,2560]{3,2,1,0:T(8,128)(2,1)} %copy.36) | data formatting | bytes 5898240 | tf_op jit(solution)/shard_map/reshape | solution.py:95
  292.9 3.3 gather_fusion
  296.2 4.5 %reshape.230 = f32[64,6,2560]{2,1,0:T(8,128)} reshape(bf16[384,2560]{1,0:T(8,128)(2,1)} %gather_fusion) | data formatting | bytes 5898240 | tf_op jit(solution)/shard_map/convert_element_type | solution.py:96
  300.7 4.4 %multiply_reduce_fusion = f32[64,2560]{1,0:T(8,128)S(1)} fusion(f32[64,6,2560]{2,1,0:T(8,128)} %reshape.230, f32[64,6]{1,0:T(8,128)S(1)} %bitcast.56), kind=kLoop, calls=%fused_computation.2 | loop fusion | flops 1802240 | bytes 4589056 | tf_op jit(solution)/shard_map/reduce_sum | solution.py:96
  305.1 2.4 convolution_add_fusion
  308.4 4.6 %all-to-all-start.1 = ((f32[4,64,640]{2,1,0:T(8,128)}), f32[4,64,640]{2,1,0:T(8,128)S(1)}, u32[]{:S(2)}, u32[]{:S(2)}) async-start(f32[4,64,640]{2,1,0:T(8,128)} %bitcast.50), calls=%async_computation.1 | async-start | bytes 1310720 | tf_op jit(solution)/shard_map/all_to_all | solution.py:14
  313.0 1.0 copy.52
  314.0 1.1 fusion.15
  315.1 25.9 %all-to-all-done.1 = f32[4,64,640]{2,1,0:T(8,128)S(1)} async-done(((f32[4,64,640]{2,1,0:T(8,128)}), f32[4,64,640]{2,1,0:T(8,128)S(1)}, u32[]{:S(2)}, u32[]{:S(2)}) %all-to-all-start.1) | async-done | bytes 655392 | tf_op jit(solution)/shard_map/all_to_all | solution.py:14
  341.0 1.9 collective-permute-start
  343.0 31.8 %all-gather.4.cloned.1.call-done = bf16[3,32,6,2560]{3,1,2,0:T(8,128)(2,1)} async-done(((bf16[3,32,6,640]{3,1,2,0:T(8,128)(2,1)}), bf16[3,32,6,2560]{3,1,2,0:T(8,128)(2,1)}) %all-gather.4.cloned.1.call-update) | async-done | bytes 2949136 | tf_op jit(solution)/shard_map/all_gather | solution.py:112
  374.8 5.1 %fusion.9 = bf16[1,3,32,6,256]{4,2,3,1,0:T(8,128)(2,1)} fusion(bf16[3,32,6,2560]{3,1,2,0:T(8,128)(2,1)} %all-gather.4.cloned.1.call-done, bf16[1,3,256,2560]{3,2,1,0:T(8,128)(2,1)} %param.12), kind=kOutput, calls=%fused_computation.12 | convolution fusion | flops 755122176 | bytes 7176192 | tf_op jit(solution)/shard_map/egmd,ehd->egmh/dot_general | solution.py:113
  (52 shorter events, 7.3 us)
Async XLA Ops:
  7.2 26.9 %copy-start = (bf16[1,3,32,6,256]{4,2,3,1,0:T(8,128)(2,1)S(1)}, bf16[1,3,32,6,256]{4,2,3,1,0:T(8,128)(2,1)}, u32[]{:S(2)}) copy-start(bf16[1,3,32,6,256]{4,2,3,1,0:T(8,128)(2,1)} %param.11) | copy-start | bytes 884740
  7.2 3.6 copy-start.5
  14.7 68.7 %all-to-all-start.2 = ((bf16[3,32,6,640]{3,2,0,1:T(8,128)(2,1)}), bf16[3,32,6,640]{3,2,0,1:T(8,128)(2,1)S(1)}, u32[]{:S(2)}, u32[]{:S(2)}) async-start(bf16[3,32,6,640]{3,2,0,1:T(8,128)(2,1)} %copy.44), calls=%async_computation.2 | async-start | bytes 1966080 | tf_op jit(solution)/shard_map/all_to_all | solution.py:105
  40.7 53.2 %copy-start.4 = (s32[1,64,6]{1,0,2:T(1,128)S(1)}, s32[1,64,6]{1,0,2:T(1,128)}, u32[]{:S(2)}) copy-start(s32[1,64,6]{1,0,2:T(1,128)} %param.9) | copy-start | bytes 4612
  40.7 233.7 %copy-start.2 = (bf16[1,64,640]{2,1,0:T(8,128)(2,1)S(1)}, bf16[1,64,640]{2,1,0:T(8,128)(2,1)}, u32[]{:S(2)}) copy-start(bf16[1,64,640]{2,1,0:T(8,128)(2,1)} %param.17) | copy-start | bytes 245764
  83.5 190.9 %all-to-all-start = ((bf16[3,32,6,2560]{3,2,0,1:T(8,128)(2,1)}), bf16[3,32,6,2560]{3,2,0,1:T(8,128)(2,1)}, u32[]{:S(2)}, u32[]{:S(2)}) async-start(bf16[3,32,6,2560]{3,2,0,1:T(8,128)(2,1)} %copy.35), calls=%async_computation | async-start | bytes 7864320 | tf_op jit(solution)/shard_map/all_to_all | solution.py:94
  92.1 192.2 %copy-start.6 = (f32[1,64,6]{1,0,2:T(1,128)S(1)}, f32[1,64,6]{1,0,2:T(1,128)}, u32[]{:S(2)}) copy-start(f32[1,64,6]{1,0,2:T(1,128)} %param.10) | copy-start | bytes 4612
  92.1 213.0 %all-gather.6.cloned.1.call-start = ((), (), s32[]{:S(2)}) async-start(), calls=%async_computation.5 | async-start | bytes 2027520 | tf_op jit(solution)/shard_map/all_gather | solution.py:86
  92.9 281.9 %all-gather.4.cloned.1.call-start = ((), (), s32[]{:S(2)}) async-start(), calls=%async_computation.4 | async-start | bytes 3686400 | tf_op jit(solution)/shard_map/all_gather | solution.py:112
  275.1 33.3 %all-to-all-start.3 = ((bf16[4,64,640]{2,1,0:T(8,128)(2,1)}), bf16[4,64,640]{2,1,0:T(8,128)(2,1)}, u32[]{:S(2)}, u32[]{:S(2)}) async-start(bf16[4,64,640]{2,1,0:T(8,128)(2,1)} %broadcast_in_dim.26), calls=%async_computation.3 | async-start | bytes 655360 | tf_op jit(solution)/shard_map/all_to_all | solution.py:26
  300.7 4.4 %copy-start.3 = (bf16[1,64,384]{2,1,0:T(8,128)(2,1)S(1)}, bf16[1,64,384]{2,1,0:T(8,128)(2,1)}, u32[]{:S(2)}) copy-start(bf16[1,64,384]{2,1,0:T(8,128)(2,1)} %param.13) | copy-start | bytes 147460
  305.1 8.9 %copy-start.1 = (bf16[1,384,2560]{1,2,0:T(8,128)(2,1)S(1)}, bf16[1,384,2560]{1,2,0:T(8,128)(2,1)}, u32[]{:S(2)}) copy-start(bf16[1,384,2560]{1,2,0:T(8,128)(2,1)} %all-gather.6.cloned.1.call-done) | copy-start | bytes 5898244
  308.4 32.6 %all-to-all-start.1 = ((f32[4,64,640]{2,1,0:T(8,128)}), f32[4,64,640]{2,1,0:T(8,128)S(1)}, u32[]{:S(2)}, u32[]{:S(2)}) async-start(f32[4,64,640]{2,1,0:T(8,128)} %bitcast.50), calls=%async_computation.1 | async-start | bytes 1310720 | tf_op jit(solution)/shard_map/all_to_all | solution.py:14
  341.0 38.9 %collective-permute-start = (bf16[64,640]{1,0:T(8,128)(2,1)S(1)}, bf16[64,640]{1,0:T(8,128)(2,1)S(1)}, u32[]{:S(2)}, u32[]{:S(2)}) collective-permute-start(bf16[64,640]{1,0:T(8,128)(2,1)S(1)} %reduce_sum.62), channel_id=1, source_target_pairs={{0,128},{128,256},{256,384},{384,0},{1,129},{129,257},{257,385},{3... | collective-permute-start | bytes 245768 | tf_op jit(solution)/shard_map/ppermute | solution.py:21
Sparse Core Ops, SparseCore 0:
  96.1 197.4 all-gather.5
  295.8 78.9 all-gather.3
where the time goes:
time: 392 us; the launch traced here: 387 us
  waiting for transfers between devices  282 us (72%)
  starting transfers between devices  42.7 us (11%)
  local copies, waits for them, and re-layouts  28.3 us (7%)
  between operations  14.3 us (4%)
  matrix products  11.7 us (3%)
  other arithmetic  8.78 us (2%)
    all_to_all x1, waiting for transfers between devices, on_device(): lax.all_to_all(partial_value, 'expert', split_axis=1, concat_axis=1, tile...  180 us
    all_to_all x1, waiting for transfers between devices, on_device(): lax.all_to_all(outgoing.reshape(experts_here, groups, capacity, local_cot...  42.7 us
    all_gather x1, waiting for transfers between devices, on_device(): received = lax.all_gather(received_part, 'tensor', axis=3, tiled=True)  31.8 us
    all_to_all x1, waiting for transfers between devices, summed_on_arrival(): lax.all_to_all(parts, axis, split_axis=0, concat_axis=0, tiled=True)  25.9 us
    all_to_all x1, starting transfers between devices, on_device(): lax.all_to_all(outgoing.reshape(experts_here, groups, capacity, local_cot...  19.4 us
    all_to_all x1, starting transfers between devices, on_device(): lax.all_to_all(partial_value, 'expert', split_axis=1, concat_axis=1, tile...  8.65 us
    all_to_all x1, starting transfers between devices, sent_to_all(): lax.all_to_all(jnp.broadcast_to(array[None], (length, *array.shape)), axi...  8.16 us
  transfers between devices with their start and end apart: 7, of which 4 were waited for; matrix products, arithmetic and copies ran while one was open for 10% of the time, Pallas kernels for 0%

commit v1 on v0

v1 whole, which is shorter than its diff:
```python
import functools

import jax
import jax.numpy as jnp
from jax import lax
from jax.experimental import pallas as pl
from jax.experimental.pallas import tpu as pltpu
from jax.sharding import Mesh, PartitionSpec as P

BF, F32 = jnp.bfloat16, jnp.float32
ZHI, YS, CORES, QS = 4, 4, 2, 4
DESTS = YS * CORES
HERE, MOST, TOK, TOP = 3, 6, 64, 6
SLOTS = ZHI * MOST
COLS = DESTS * HERE
ROWS = COLS * SLOTS
FEAT, HID = 640, 256
HSQ, WCOL = 384, 80
TALL = ZHI * TOK
XPAD = 32
BLOCKS = HERE * QS + 2
WIDE = FEAT + HSQ + 128
SEND = FEAT + HSQ
VM = pl.BlockSpec(memory_space=pltpu.VMEM)


def call(body, outs, args, flops=0, name=None):
    out_shape = [jax.ShapeDtypeStruct(s, t) for s, t in outs]
    size = sum(a.size * a.dtype.itemsize for a in (*args, *out_shape))
    return pl.pallas_call(
        body,
        out_shape=out_shape,
        in_specs=[VM] * len(args),
        out_specs=[VM] * len(outs),
        cost_estimate=pl.CostEstimate(flops=flops, bytes_accessed=size, transcendentals=0),
        compiler_params=pltpu.CompilerParams(vmem_limit_bytes=48 * 2**20),
        name=name,
    )(*args)


def iota(shape, dim):
    return lax.broadcasted_iota(jnp.int32, shape, dim)


def dot(a, b, dims=((1,), (0,))):
    return lax.dot_general(a, b, (dims, ((), ())), preferred_element_type=F32)


def split_row(r):
    x = (r * 2731) >> 16
    rest = r - x * SLOTS
    group = (rest * 43) >> 8
    return x, group, rest - group * MOST


def fore_kernel(hidden, weight, columns, out, rows_ref):
    step = pl.program_id(0)
    count = MOST * ZHI * DESTS

    @pl.when((step < 2 * HERE) & (lax.rem(step, 2) == 0))
    def _():
        to, src = iota((count, count), 0), iota((count, count), 1)
        slot, group = src >> 5, src & 31
        zhi, dest = group >> 3, group & 7
        perm = jnp.where(to == (dest * SLOTS + zhi * MOST + slot), 1.0, 0.0).astype(BF)
        rows_ref[...] = dot(perm, hidden[0].reshape(count, HID)).astype(BF)

    @pl.when(step < 2 * HERE)
    def _():
        for q in range(2):
            value = dot(rows_ref[...], weight[0, :, q * FEAT : (q + 1) * FEAT])
            out[:, q] = value.reshape(DESTS, SLOTS, FEAT).astype(BF)

    @pl.when(step == 2 * HERE)
    def _():
        wide = columns[...].astype(F32)
        tiles = [wide[8 * m : 8 * m + 8, 128 * i : 128 * i + 128] for i in range(3) for m in range(10)]
        for b in range(2):
            lanes = [jnp.concatenate(tiles[3 * n : 3 * n + 3], axis=0) for n in range(5 * b, 5 * b + 5)]
            block = jnp.concatenate(lanes, axis=1).astype(BF)
            for d in range(DESTS):
                out[d, b] = block


def unpacked_columns(rows):
    pieces = []
    for d in range(DESTS):
        blocks = [rows[d, BLOCKS - 2 + b].astype(F32) for b in range(2)]
        tiles = [
            blocks[n // 5][8 * m : 8 * m + 8, 128 * (n % 5) : 128 * (n % 5) + 128]
            for n in range(10)
            for m in range(3)
        ]
        lanes = [jnp.concatenate(tiles[10 * i : 10 * i + 10], axis=0) for i in range(3)]
        pieces.append(jnp.concatenate(lanes, axis=1))
    return jnp.concatenate(pieces, axis=0).astype(BF)


def back_kernel(rows, weight, out):
    count = MOST * ZHI * DESTS
    total = jnp.zeros((count, HID), F32)
    for q in range(QS):
        piece = rows[:, 0, q].astype(F32).reshape(count, FEAT).astype(BF)
        total += dot(piece, weight[0, :, q * FEAT : (q + 1) * FEAT], ((1,), (1,)))
    to, src = iota((count, count), 0), iota((count, count), 1)
    slot, group = to >> 5, to & 31
    zhi, dest = group >> 3, group & 7
    perm = jnp.where(src == (dest * SLOTS + zhi * MOST + slot), 1.0, 0.0).astype(BF)
    value = dot(perm, total.astype(BF)).astype(BF)
    out[0] = value.reshape(MOST, ZHI * DESTS, HID)


def select_kernel(whole, cot0, cot1, cot2, cot3, out):
    q = lax.axis_index("tensor")
    meta = whole[:, :, SEND:].astype(F32).reshape(TALL, 128).T
    names = iota((XPAD, TALL), 0) + lax.axis_index("zhi") * COLS
    hit = jnp.zeros((XPAD, TALL), F32)
    gates = [jnp.zeros((XPAD, TALL), F32) for _ in range(3)]
    for k in range(TOP):
        found = jnp.where(meta[6 + k : 7 + k, :].astype(jnp.int32) == names, 1.0, 0.0)
        hit += found
        for i in range(3):
            gates[i] += found * meta[30 + 6 * i + k : 31 + 6 * i + k, :]
    a, b = iota((TALL, TALL), 0), iota((TALL, TALL), 1)
    before = jnp.where((a < b) & ((a >> 6) == (b >> 6)), 1.0, 0.0).astype(BF)
    slot = jnp.where(hit > 0, dot(hit.astype(BF), before), 100.0)
    x, _, _ = split_row(iota((ROWS, XPAD), 0))
    spread = jnp.where(x == iota((ROWS, XPAD), 1), 1.0, 0.0).astype(BF)
    slots = dot(spread, slot.astype(BF))
    gate = sum(dot(spread, g.astype(BF)) for g in gates)
    _, group, want = split_row(iota((ROWS, TALL), 0))
    chosen = (slots == want.astype(F32)) & (group == (iota((ROWS, TALL), 1) >> 6))
    pick = jnp.where(chosen, 1.0, 0.0).astype(BF)
    scale = jnp.sum(jnp.where(chosen, gate, 0.0), axis=1, keepdims=True)
    for i, cot in enumerate((cot0, cot1, cot2, cot3)):
        value = dot(pick, cot[...].reshape(TALL, FEAT)) * scale
        out[:, :, lax.rem(q + i, QS)] = value.reshape(DESTS, HERE, SLOTS, FEAT).astype(BF)


def combine_kernel(whole, rows, own, send1, send2, send3, columns):
    me = lax.axis_index("zhi")
    q = lax.axis_index("tensor")
    meta = whole[:, :, SEND:].astype(F32).reshape(TALL, 128)
    names = iota((TALL, 128), 1) + me * COLS
    hit = jnp.zeros((TALL, 128), F32)
    gates = [jnp.zeros((TALL, 128), F32) for _ in range(3)]
    for k in range(TOP):
        found = jnp.where(meta[:, k : k + 1].astype(jnp.int32) == names, 1.0, 0.0)
        hit += found
        for i in range(3):
            gates[i] += found * meta[:, 12 + 6 * i + k : 13 + 6 * i + k]
    a, b = iota((TALL, TALL), 0), iota((TALL, TALL), 1)
    before = jnp.where((b < a) & ((a >> 6) == (b >> 6)), 1.0, 0.0).astype(BF)
    slot = jnp.where(hit > 0, dot(before, hit.astype(BF)), 100.0)
    x, _, _ = split_row(iota((128, ROWS), 1))
    spread = jnp.where(x == iota((128, ROWS), 0), 1.0, 0.0).astype(BF)
    slots = dot(slot.astype(BF), spread)
    _, group, want = split_row(iota((TALL, ROWS), 1))
    chosen = (slots == want.astype(F32)) & (group == (iota((TALL, ROWS), 0) >> 6))
    mix = [jnp.where(chosen, dot(g.astype(BF), spread), 0.0).astype(BF) for g in gates]
    mix = jnp.concatenate(mix, axis=0)
    mine = unpacked_columns(rows)
    columns[...] = mine
    hidden = whole[:, :, FEAT:SEND].reshape(TALL, HSQ)
    shared = dot(hidden, mine, ((1,), (1,)))
    for i, out in enumerate((own, send1, send2, send3)):
        at = lax.rem(q + i, QS)
        piece = jnp.concatenate(
            [
                rows[d, e * QS + at].astype(F32)
                for d in range(DESTS)
                for e in range(HERE)
            ],
            axis=0,
        ).astype(BF)
        value = dot(mix, piece)
        value = value[:TALL] + value[TALL : 2 * TALL] + value[2 * TALL :]
        value += jnp.where(at == me, shared, 0.0)
        out[...] = value.reshape(ZHI, TOK, FEAT).astype(BF)


def zsum_kernel(got0, got1, got2, got3, columns, cot0, cot1, cot2, cot3, own, *outs):
    me = lax.axis_index("zhi")
    q = lax.axis_index("tensor")
    where = lax.rem(me - q + QS, QS)
    for k in range(ZHI):
        at = lax.rem(me + k, ZHI)
        value = sum(got[at].astype(F32) for got in (got0, got1, got2, got3))
        out = own if k == 0 else outs[k - 1]
        out[:, :FEAT] = value.astype(out.dtype)
    for i, cot in enumerate((cot0, cot1, cot2, cot3)):

        @pl.when(where == i)
        def _(cot=cot):
            for k in range(ZHI):
                out = own if k == 0 else outs[k - 1]
                part = dot(cot[lax.rem(me + k, ZHI)], columns[...])
                out[:, FEAT:] = part.astype(out.dtype)


def last_kernel(own, got1, got2, got3, layer, grad):
    value = own[...] + got1[...].astype(F32) + got2[...].astype(F32) + got3[...].astype(F32)
    layer[...] = value[:, :FEAT].astype(BF)
    grad[...] = value[:, FEAT:].astype(BF)


def moved(value, axes, count, step):
    return lax.ppermute(value, axes, [(i, (i + step) % count) for i in range(count)])


def z_pairs(step):
    total = ZHI * QS
    if step == 2:
        return [(z, (z + (2 if z % 2 == 0 else -2)) % total) for z in range(total)]
    return [(z, (z + step) % total) for z in range(total)]


def over_z(value, step):
    return lax.ppermute(value, ("zhi", "tensor"), z_pairs(step))


def over_z_and_phase(value, step):
    total = ZHI * QS
    pairs = [
        (p * total + a, (p + 1) % 4 * total + b) for p in range(4) for a, b in z_pairs(step)
    ]
    return lax.ppermute(value, ("phase", "zhi", "tensor"), pairs)


def bf16_parts(gates):
    first = lax.reduce_precision(gates, 8, 7)
    rest = gates - first
    second = lax.reduce_precision(rest, 8, 7)
    return [first, second, rest - second]


def on_device(
    forward_routes,
    forward_gates,
    hidden_rows,
    down_weight,
    shared_hidden,
    shared_weight,
    backward_routes,
    backward_gates,
    cotangent,
):
    weight = down_weight[0]
    cot = cotangent[0]
    meta = jnp.concatenate(
        [forward_routes[0].T.astype(F32), backward_routes[0].T.astype(F32)]
        + bf16_parts(forward_gates[0].T)
        + bf16_parts(backward_gates[0].T),
        axis=0,
    ).astype(BF)
    meta = jnp.pad(meta.T, ((0, 0), (0, 128 - 8 * TOP)))
    packed = jnp.concatenate([cot, shared_hidden[0], meta], axis=1)

    hidden = jnp.transpose(hidden_rows[0], (0, 2, 1, 3))
    parts = pl.pallas_call(
        fore_kernel,
        grid=(2 * HERE + 1,),
        in_specs=[
            pl.BlockSpec((1, MOST, ZHI * DESTS, HID), lambda i: (jnp.minimum(i // 2, 2), 0, 0, 0)),
            pl.BlockSpec(
                (1, HID, 2 * FEAT),
                lambda i: (jnp.minimum(i // 2, 2), 0, jnp.where(i < 6, lax.rem(i, 2), 1)),
            ),
            pl.BlockSpec((WCOL, HSQ), lambda i: (0, 0)),
        ],
        out_specs=pl.BlockSpec((DESTS, 2, SLOTS, FEAT), lambda i: (0, i, 0, 0)),
        out_shape=jax.ShapeDtypeStruct((DESTS, BLOCKS, SLOTS, FEAT), BF),
        scratch_shapes=[pltpu.VMEM((MOST * ZHI * DESTS, HID), BF)],
        cost_estimate=pl.CostEstimate(
            flops=2 * HERE * 192 * HID * FEAT * QS, bytes_accessed=8 * 10**6, transcendentals=0
        ),
        compiler_params=pltpu.CompilerParams(vmem_limit_bytes=40 * 2**20),
        name="expert_rows",
    )(hidden, weight, shared_weight[0].T)
    arrived = lax.all_to_all(parts, ("y", "core"), 0, 0, tiled=True)

    packed, parts = lax.optimization_barrier((packed, parts))
    whole = lax.all_gather(packed, "zhi", axis=0, tiled=False)
    held = whole[:, :, :FEAT]
    chunks = [held, over_z(held, -1), over_z(held, 2), over_z(held, 1)]
    [outgoing] = call(
        select_kernel,
        [((DESTS, HERE, QS, SLOTS, FEAT), BF)],
        [whole, *chunks],
        flops=2 * ROWS * TALL * FEAT * QS,
        name="select_rows",
    )
    received = lax.all_to_all(outgoing, ("y", "core"), 0, 0, tiled=True)

    chunk = ((ZHI, TOK, FEAT), BF)
    *sends, columns = call(
        combine_kernel,
        [chunk, chunk, chunk, chunk, ((FEAT, HSQ), BF)],
        [whole, arrived],
        flops=6 * TALL * ROWS * FEAT * QS,
        name="combine",
    )
    got = [over_z_and_phase(value, step) for value, step in zip(sends, (0, 1, 2, -1))]
    own, *sums = call(
        zsum_kernel,
        [((TOK, SEND), F32)] + [((TOK, SEND), BF)] * 3,
        [*got, columns, *chunks],
        name="z_sum",
    )
    last = [moved(value, "zhi", ZHI, k) for k, value in zip((1, 2, 3), sums)]
    handed, shared_back = call(
        last_kernel, [((TOK, FEAT), BF), ((TOK, HSQ), BF)], [own, *last], name="last_sum"
    )

    hidden_back = pl.pallas_call(
        back_kernel,
        grid=(HERE,),
        in_specs=[
            pl.BlockSpec((DESTS, 1, QS, SLOTS, FEAT), lambda e: (0, e, 0, 0, 0)),
            pl.BlockSpec((1, HID, FEAT * QS), lambda e: (e, 0, 0)),
        ],
        out_specs=pl.BlockSpec((1, MOST, ZHI * DESTS, HID), lambda e: (e, 0, 0, 0)),
        out_shape=jax.ShapeDtypeStruct((HERE, MOST, ZHI * DESTS, HID), BF),
        cost_estimate=pl.CostEstimate(
            flops=2 * HERE * 192 * HID * FEAT * QS, bytes_accessed=7 * 10**6, transcendentals=0
        ),
        compiler_params=pltpu.CompilerParams(vmem_limit_bytes=40 * 2**20),
        name="hidden_back",
    )(received, weight)
    return (
        handed[None],
        jnp.transpose(hidden_back, (0, 2, 1, 3))[None],
        shared_back[None],
    )


def solution(mesh):
    inner = Mesh(
        mesh.devices.reshape(4, ZHI, YS, CORES, QS), ("phase", "zhi", "y", "core", "tensor")
    )
    expert = ("zhi", "y", "core")
    return jax.shard_map(
        on_device,
        mesh=inner,
        in_specs=(
            P("phase", expert, None),
            P("phase", expert, None),
            P("phase", expert, None, None, "tensor"),
            P("phase", expert, "tensor", None),
            P("phase", expert, "tensor"),
            P("phase", "tensor", expert),
            P("phase", expert, None),
            P("phase", expert, None),
            P("phase", expert, "tensor"),
        ),
        out_specs=(
            P("phase", expert, "tensor"),
            P("phase", expert, None, None, "tensor"),
            P("phase", expert, "tensor"),
        ),
        check_vma=False,
    )
```

time: 392 us -> 164 us (0.42)
  the two profiles are of different devices: /device:TPU:1 before, /device:TPU:65 now
where the time goes in v1:
time: 164 us; the launch traced here: 163 us
  starting transfers between devices  55.5 us (34%)
  waiting for transfers between devices  46.2 us (28%)
  blocking collectives  29.9 us (18%)
  Pallas kernels  21.4 us (13%)
  local copies, waits for them, and re-layouts  9.54 us (6%)
    all_gather x1, blocking collectives, on_device(): whole = lax.all_gather(packed, 'zhi', axis=0, tiled=False)  29.9 us
    ppermute x3, waiting for transfers between devices, moved(): lax.ppermute(value, axes, [(i, (i + step) % count) for i in range(count)])  19.8 us
    ppermute x4, waiting for transfers between devices, over_z_and_phase(): return lax.ppermute(value, ('phase', 'zhi', 'tensor'), pairs)  18.3 us
    ppermute x3, starting transfers between devices, moved(): lax.ppermute(value, axes, [(i, (i + step) % count) for i in range(count)])  15.9 us
    ppermute x4, starting transfers between devices, over_z_and_phase(): return lax.ppermute(value, ('phase', 'zhi', 'tensor'), pairs)  15.2 us
    pallas_call x4, Pallas kernels, call(): pl.pallas_call(body, out_shape=out_shape, in_specs=[VM] * len(args), out_...  13.1 us
    ppermute x3, starting transfers between devices, over_z(): return lax.ppermute(value, ('zhi', 'tensor'), z_pairs(step))  10.7 us
    unnamed x37, local copies, waits for them, and re-layouts  9.08 us
  transfers between devices with their start and end apart: 12, of which 5 were waited for; matrix products, arithmetic and copies ran while one was open for 0% of the time, Pallas kernels for 9%

profile of v1, /device:TPU:65, one launch (start us, length us, event | category | flops | bytes accessed | tf_op | source)
XLA Modules:
  0.0 163.4 jit_solution(3740595259675181501)
XLA Ops:
  0.6 2.1 %copy-done = bf16[1,3,256,2560]{3,2,1,0:T(8,128)(2,1)S(1)} copy-done((bf16[1,3,256,2560]{3,2,1,0:T(8,128)(2,1)S(1)}, bf16[1,3,256,2560]{3,2,1,0:T(8,128)(2,1)}, u32[]{:S(2)}) %copy-start) | copy-done | bytes 3932184
  4.5 5.0 %expert_rows.1 = bf16[8,14,24,640]{3,2,1,0:T(8,128)(2,1)} custom-call(bf16[3,6,32,256]{3,2,1,0:T(8,128)(2,1)S(1)} %bitcast.47, bf16[3,256,2560]{2,1,0:T(8,128)(2,1)S(1)} %bitcast.42, bf16[80,384]{1,0:T(8,128)(2,1)S(1)} %bitcast.48), custom_call_target="tpu_custom_call" | custom-call | flops 754974720 | bytes 8000000 | tf_op jit(solution)/shard_map/expert_rows/pallas_call | solution.py:260
  9.6 5.3 %all-to-all-start = ((bf16[8,14,24,640]{3,2,1,0:T(8,128)(2,1)}), bf16[8,14,24,640]{3,2,1,0:T(8,128)(2,1)}, u32[]{:S(2)}, u32[]{:S(2)}) async-start(bf16[8,14,24,640]{3,2,1,0:T(8,128)(2,1)} %expert_rows.1), calls=%async_computation | async-start | bytes 6881280 | tf_op jit(solution)/shard_map/all_to_all | solution.py:280
  15.5 29.9 %all-gather = bf16[256,1152]{1,0:T(8,128)(2,1)S(1)} all-gather(bf16[64,1152]{1,0:T(8,128)(2,1)S(1)} %fusion.1), channel_id=2, replica_groups=mesh['phase'=4,'zhi'=4,'y'=4,'core'=2,'tensor'=4] {'zhi'}, dimensions={0}, use_global_device_ids=true | all-gather | bytes 737280 | tf_op jit(solution)/shard_map/all_gather | solution.py:283
  45.4 4.1 %collective-permute-start.6 = (bf16[4,64,640]{2,1,0:T(8,128)(2,1)S(1)}, bf16[4,64,640]{2,1,0:T(8,128)(2,1)S(1)}, u32[]{:S(2)}, u32[]{:S(2)}) collective-permute-start(bf16[4,64,640]{2,1,0:T(8,128)(2,1)S(1)} %slice.4.cot0), channel_id=1, source_target_pairs={{0,1},{1,2},{2,3},{3,32},{32,33},{33,34},{34,35},{35,64},{64,65},{... | collective-permute-start | bytes 983048 | tf_op jit(solution)/shard_map/ppermute | solution.py:219
  49.5 2.6 %collective-permute-start.5 = (bf16[4,64,640]{2,1,0:T(8,128)(2,1)S(1)}, bf16[4,64,640]{2,1,0:T(8,128)(2,1)S(1)}, u32[]{:S(2)}, u32[]{:S(2)}) collective-permute-start(bf16[4,64,640]{2,1,0:T(8,128)(2,1)S(1)} %slice.4.cot0), channel_id=1, source_target_pairs={{0,2},{1,99},{2,32},{3,1},{32,34},{33,3},{34,64},{35,33},{64,66},{... | collective-permute-start | bytes 983048 | tf_op jit(solution)/shard_map/ppermute | solution.py:219
  52.1 4.1 %collective-permute-start.4 = (bf16[4,64,640]{2,1,0:T(8,128)(2,1)S(1)}, bf16[4,64,640]{2,1,0:T(8,128)(2,1)S(1)}, u32[]{:S(2)}, u32[]{:S(2)}) collective-permute-start(bf16[4,64,640]{2,1,0:T(8,128)(2,1)S(1)} %slice.4.cot0), channel_id=1, source_target_pairs={{0,99},{1,0},{2,1},{3,2},{32,3},{33,32},{34,33},{35,34},{64,35},{6... | collective-permute-start | bytes 983048 | tf_op jit(solution)/shard_map/ppermute | solution.py:219
  56.1 4.7 %collective-permute-done.5.cot2 = bf16[4,64,640]{2,1,0:T(8,128)(2,1)S(1)} collective-permute-done((bf16[4,64,640]{2,1,0:T(8,128)(2,1)S(1)}, bf16[4,64,640]{2,1,0:T(8,128)(2,1)S(1)}, u32[]{:S(2)}, u32[]{:S(2)}) %collective-permute-start.5) | collective-permute-done | bytes 327712 | tf_op jit(solution)/shard_map/ppermute | solution.py:219
  60.9 3.4 %collective-permute-done.4.cot1 = bf16[4,64,640]{2,1,0:T(8,128)(2,1)S(1)} collective-permute-done((bf16[4,64,640]{2,1,0:T(8,128)(2,1)S(1)}, bf16[4,64,640]{2,1,0:T(8,128)(2,1)S(1)}, u32[]{:S(2)}, u32[]{:S(2)}) %collective-permute-start.4) | collective-permute-done | bytes 327712 | tf_op jit(solution)/shard_map/ppermute | solution.py:219
  64.2 3.3 %select_rows.1 = bf16[8,3,4,24,640]{4,3,2,1,0:T(8,128)(2,1)} custom-call(bf16[4,64,1152]{2,1,0:T(8,128)(2,1)S(1)} %bitcast.45, bf16[4,64,640]{2,1,0:T(8,128)(2,1)S(1)} %slice.4.cot0, bf16[4,64,640]{2,1,0:T(8,128)(2,1)S(1)} %collective-permute-done.4.cot1, bf16[4,64,640]{2,1,0:T(8,128)(2,1)S(1)} %collective-permute-done.5.cot2, ...), custom_call_target="tpu_custom_call" | custom-call | flops 754974720 | bytes 4849664 | tf_op jit(solution)/shard_map/select_rows/pallas_call | solution.py:30
  70.4 8.5 %all-to-all-start.1 = ((bf16[8,3,4,24,640]{4,3,2,1,0:T(8,128)(2,1)}), bf16[8,3,4,24,640]{4,3,2,1,0:T(8,128)(2,1)S(1)}, u32[]{:S(2)}, u32[]{:S(2)}) async-start(bf16[8,3,4,24,640]{4,3,2,1,0:T(8,128)(2,1)} %select_rows.1), calls=%async_computation.1 | async-start | bytes 5898240 | tf_op jit(solution)/shard_map/all_to_all | solution.py:293
  78.9 6.9 %combine.1 = (bf16[4,64,640]{2,1,0:T(8,128)(2,1)S(1)}, bf16[4,64,640]{2,1,0:T(8,128)(2,1)S(1)}, bf16[4,64,640]{2,1,0:T(8,128)(2,1)S(1)}, bf16[4,64,640]{2,1,0:T(8,128)(2,1)S(1)}, bf16[640,384]{1,0:T(8,128)(2,1)S(1)}) custom-call(bf16[4,64,1152]{2,1,0:T(8,128)(2,1)S(1)} %bitcast.46, bf16[8,14,24,640]{3,2,1,0:T(8,128)(2,1)} %all-to-all-done.rows), custom_call_target="tpu_custom_call" | custom-call | flops 2264924160 | bytes 5832704 | tf_op jit(solution)/shard_map/combine/pallas_call | solution.py:30
  85.8 3.1 %collective-permute-start = (bf16[4,64,640]{2,1,0:T(8,128)(2,1)S(1)}, bf16[4,64,640]{2,1,0:T(8,128)(2,1)S(1)}, u32[]{:S(2)}, u32[]{:S(2)}) collective-permute-start(bf16[4,64,640]{2,1,0:T(8,128)(2,1)S(1)} %get-tuple-element.16), channel_id=1, source_target_pairs={{0,128},{1,129},{2,130},{3,131},{32,160},{33,161},{34,162},{35,163... | collective-permute-start | bytes 983048 | tf_op jit(solution)/shard_map/ppermute | solution.py:227
  88.9 6.4 %collective-permute-start.1 = (bf16[4,64,640]{2,1,0:T(8,128)(2,1)S(1)}, bf16[4,64,640]{2,1,0:T(8,128)(2,1)S(1)}, u32[]{:S(2)}, u32[]{:S(2)}) collective-permute-start(bf16[4,64,640]{2,1,0:T(8,128)(2,1)S(1)} %get-tuple-element.17), channel_id=1, source_target_pairs={{0,129},{1,130},{2,131},{3,160},{32,161},{33,162},{34,163},{35,192... | collective-permute-start | bytes 983048 | tf_op jit(solution)/shard_map/ppermute | solution.py:227
  95.3 2.5 %collective-permute-start.2 = (bf16[4,64,640]{2,1,0:T(8,128)(2,1)S(1)}, bf16[4,64,640]{2,1,0:T(8,128)(2,1)S(1)}, u32[]{:S(2)}, u32[]{:S(2)}) collective-permute-start(bf16[4,64,640]{2,1,0:T(8,128)(2,1)S(1)} %get-tuple-element.18), channel_id=1, source_target_pairs={{0,130},{1,227},{2,160},{3,129},{32,162},{33,131},{34,192},{35,161... | collective-permute-start | bytes 983048 | tf_op jit(solution)/shard_map/ppermute | solution.py:227
  97.8 3.2 %collective-permute-start.3 = (bf16[4,64,640]{2,1,0:T(8,128)(2,1)S(1)}, bf16[4,64,640]{2,1,0:T(8,128)(2,1)S(1)}, u32[]{:S(2)}, u32[]{:S(2)}) collective-permute-start(bf16[4,64,640]{2,1,0:T(8,128)(2,1)S(1)} %get-tuple-element.19), channel_id=1, source_target_pairs={{0,227},{1,128},{2,129},{3,130},{32,131},{33,160},{34,161},{35,162... | collective-permute-start | bytes 983048 | tf_op jit(solution)/shard_map/ppermute | solution.py:227
  101.0 18.3 %collective-permute-done.got0 = bf16[4,64,640]{2,1,0:T(8,128)(2,1)S(1)} collective-permute-done((bf16[4,64,640]{2,1,0:T(8,128)(2,1)S(1)}, bf16[4,64,640]{2,1,0:T(8,128)(2,1)S(1)}, u32[]{:S(2)}, u32[]{:S(2)}) %collective-permute-start) | collective-permute-done | bytes 327712 | tf_op jit(solution)/shard_map/ppermute | solution.py:227
  120.8 4.4 %collective-permute-start.7 = (bf16[64,1024]{1,0:T(8,128)(2,1)}, bf16[64,1024]{1,0:T(8,128)(2,1)S(1)}, u32[]{:S(2)}, u32[]{:S(2)}) collective-permute-start(bf16[64,1024]{1,0:T(8,128)(2,1)} %get-tuple-element.22), channel_id=1, source_target_pairs={{0,32},{32,64},{64,96},{96,0},{1,33},{33,65},{65,97},{97,1},{2,34}... | collective-permute-start | bytes 393224 | tf_op jit(solution)/shard_map/ppermute | solution.py:208
  125.1 7.3 %collective-permute-start.8 = (bf16[64,1024]{1,0:T(8,128)(2,1)}, bf16[64,1024]{1,0:T(8,128)(2,1)S(1)}, u32[]{:S(2)}, u32[]{:S(2)}) collective-permute-start(bf16[64,1024]{1,0:T(8,128)(2,1)} %get-tuple-element.23), channel_id=1, source_target_pairs={{0,64},{32,96},{64,0},{96,32},{1,65},{33,97},{65,1},{97,33},{2,66}... | collective-permute-start | bytes 393224 | tf_op jit(solution)/shard_map/ppermute | solution.py:208
  132.4 4.3 %collective-permute-start.9 = (bf16[64,1024]{1,0:T(8,128)(2,1)}, bf16[64,1024]{1,0:T(8,128)(2,1)}, u32[]{:S(2)}, u32[]{:S(2)}) collective-permute-start(bf16[64,1024]{1,0:T(8,128)(2,1)} %get-tuple-element.24), channel_id=1, source_target_pairs={{0,96},{32,0},{64,32},{96,64},{1,97},{33,1},{65,33},{97,65},{2,98}... | collective-permute-start | bytes 393224 | tf_op jit(solution)/shard_map/ppermute | solution.py:208
  136.7 2.1 %copy-done.1 = bf16[1,3,256,2560]{3,2,1,0:T(8,128)(2,1)S(1)} copy-done((bf16[1,3,256,2560]{3,2,1,0:T(8,128)(2,1)S(1)}, bf16[1,3,256,2560]{3,2,1,0:T(8,128)(2,1)}, u32[]{:S(2)}) %copy-start.1) | copy-done | bytes 3932184
  138.8 3.3 %hidden_back.1 = bf16[3,6,32,256]{3,2,1,0:T(8,128)(2,1)} custom-call(bf16[8,3,4,24,640]{4,3,2,1,0:T(8,128)(2,1)S(1)} %all-to-all-done.1.rows, bf16[3,256,2560]{2,1,0:T(8,128)(2,1)S(1)} %bitcast.43), custom_call_target="tpu_custom_call" | custom-call | flops 754974720 | bytes 7000000 | tf_op jit(solution)/shard_map/hidden_back/pallas_call | solution.py:315
  142.1 8.7 %collective-permute-done.8.got2 = bf16[64,1024]{1,0:T(8,128)(2,1)S(1)} collective-permute-done((bf16[64,1024]{1,0:T(8,128)(2,1)}, bf16[64,1024]{1,0:T(8,128)(2,1)S(1)}, u32[]{:S(2)}, u32[]{:S(2)}) %collective-permute-start.8) | collective-permute-done | bytes 131104 | tf_op jit(solution)/shard_map/ppermute | solution.py:208
  150.8 11.0 %collective-permute-done.9.got3 = bf16[64,1024]{1,0:T(8,128)(2,1)} collective-permute-done((bf16[64,1024]{1,0:T(8,128)(2,1)}, bf16[64,1024]{1,0:T(8,128)(2,1)}, u32[]{:S(2)}, u32[]{:S(2)}) %collective-permute-start.9) | collective-permute-done | bytes 131104 | tf_op jit(solution)/shard_map/ppermute | solution.py:208
  (49 shorter events, 8.3 us)
Async XLA Ops:
  0.6 2.1 %copy-start = (bf16[1,3,256,2560]{3,2,1,0:T(8,128)(2,1)S(1)}, bf16[1,3,256,2560]{3,2,1,0:T(8,128)(2,1)}, u32[]{:S(2)}) copy-start(bf16[1,3,256,2560]{3,2,1,0:T(8,128)(2,1)} %param.12) | copy-start | bytes 11796484
  9.6 5.3 %copy-start.16 = (s32[1,64,6]{1,0,2:T(1,128)S(1)}, s32[1,64,6]{1,0,2:T(1,128)}, u32[]{:S(2)}) copy-start(s32[1,64,6]{1,0,2:T(1,128)} %param.9) | copy-start | bytes 4612
  9.6 5.3 %copy-start.17 = (s32[1,64,6]{1,0,2:T(1,128)S(1)}, s32[1,64,6]{1,0,2:T(1,128)}, u32[]{:S(2)}) copy-start(s32[1,64,6]{1,0,2:T(1,128)} %param.15) | copy-start | bytes 4612
  9.6 5.3 %copy-start.14 = (f32[1,64,6]{1,0,2:T(1,128)S(1)}, f32[1,64,6]{1,0,2:T(1,128)}, u32[]{:S(2)}) copy-start(f32[1,64,6]{1,0,2:T(1,128)} %param.10) | copy-start | bytes 4612
  9.6 5.3 %copy-start.15 = (f32[1,64,6]{1,0,2:T(1,128)S(1)}, f32[1,64,6]{1,0,2:T(1,128)}, u32[]{:S(2)}) copy-start(f32[1,64,6]{1,0,2:T(1,128)} %param.16) | copy-start | bytes 4612
  9.6 5.9 %copy-start.12 = (bf16[1,64,640]{2,1,0:T(8,128)(2,1)S(1)}, bf16[1,64,640]{2,1,0:T(8,128)(2,1)}, u32[]{:S(2)}) copy-start(bf16[1,64,640]{2,1,0:T(8,128)(2,1)} %param.17) | copy-start | bytes 245764
  9.6 5.9 %copy-start.13 = (bf16[1,64,384]{2,1,0:T(8,128)(2,1)S(1)}, bf16[1,64,384]{2,1,0:T(8,128)(2,1)}, u32[]{:S(2)}) copy-start(bf16[1,64,384]{2,1,0:T(8,128)(2,1)} %param.13) | copy-start | bytes 147460
  9.6 60.8 %all-to-all-start = ((bf16[8,14,24,640]{3,2,1,0:T(8,128)(2,1)}), bf16[8,14,24,640]{3,2,1,0:T(8,128)(2,1)}, u32[]{:S(2)}, u32[]{:S(2)}) async-start(bf16[8,14,24,640]{3,2,1,0:T(8,128)(2,1)} %expert_rows.1), calls=%async_computation | async-start | bytes 6881280 | tf_op jit(solution)/shard_map/all_to_all | solution.py:280
  45.4 10.7 %collective-permute-start.6 = (bf16[4,64,640]{2,1,0:T(8,128)(2,1)S(1)}, bf16[4,64,640]{2,1,0:T(8,128)(2,1)S(1)}, u32[]{:S(2)}, u32[]{:S(2)}) collective-permute-start(bf16[4,64,640]{2,1,0:T(8,128)(2,1)S(1)} %slice.4.cot0), channel_id=1, source_target_pairs={{0,1},{1,2},{2,3},{3,32},{32,33},{33,34},{34,35},{35,64},{64,65},{... | collective-permute-start | bytes 983048 | tf_op jit(solution)/shard_map/ppermute | solution.py:219
  49.5 11.4 %collective-permute-start.5 = (bf16[4,64,640]{2,1,0:T(8,128)(2,1)S(1)}, bf16[4,64,640]{2,1,0:T(8,128)(2,1)S(1)}, u32[]{:S(2)}, u32[]{:S(2)}) collective-permute-start(bf16[4,64,640]{2,1,0:T(8,128)(2,1)S(1)} %slice.4.cot0), channel_id=1, source_target_pairs={{0,2},{1,99},{2,32},{3,1},{32,34},{33,3},{34,64},{35,33},{64,66},{... | collective-permute-start | bytes 983048 | tf_op jit(solution)/shard_map/ppermute | solution.py:219
  52.1 12.2 %collective-permute-start.4 = (bf16[4,64,640]{2,1,0:T(8,128)(2,1)S(1)}, bf16[4,64,640]{2,1,0:T(8,128)(2,1)S(1)}, u32[]{:S(2)}, u32[]{:S(2)}) collective-permute-start(bf16[4,64,640]{2,1,0:T(8,128)(2,1)S(1)} %slice.4.cot0), channel_id=1, source_target_pairs={{0,99},{1,0},{2,1},{3,2},{32,3},{33,32},{34,33},{35,34},{64,35},{6... | collective-permute-start | bytes 983048 | tf_op jit(solution)/shard_map/ppermute | solution.py:219
  70.4 66.3 %all-to-all-start.1 = ((bf16[8,3,4,24,640]{4,3,2,1,0:T(8,128)(2,1)}), bf16[8,3,4,24,640]{4,3,2,1,0:T(8,128)(2,1)S(1)}, u32[]{:S(2)}, u32[]{:S(2)}) async-start(bf16[8,3,4,24,640]{4,3,2,1,0:T(8,128)(2,1)} %select_rows.1), calls=%async_computation.1 | async-start | bytes 5898240 | tf_op jit(solution)/shard_map/all_to_all | solution.py:293
  78.9 40.4 %copy-start.3 = (bf16[4,64,640]{2,1,0:T(8,128)(2,1)S(1)}, bf16[4,64,640]{2,1,0:T(8,128)(2,1)}, u32[]{:S(2)}) copy-start(bf16[4,64,640]{2,1,0:T(8,128)(2,1)} %copy-done.2) | copy-start | bytes 983044
  78.9 40.4 %copy-start.5 = (bf16[4,64,640]{2,1,0:T(8,128)(2,1)S(1)}, bf16[4,64,640]{2,1,0:T(8,128)(2,1)}, u32[]{:S(2)}) copy-start(bf16[4,64,640]{2,1,0:T(8,128)(2,1)} %copy-done.4) | copy-start | bytes 983044
  78.9 40.5 %copy-start.7 = (bf16[4,64,640]{2,1,0:T(8,128)(2,1)S(1)}, bf16[4,64,640]{2,1,0:T(8,128)(2,1)}, u32[]{:S(2)}) copy-start(bf16[4,64,640]{2,1,0:T(8,128)(2,1)} %copy-done.6) | copy-start | bytes 983044
  78.9 40.5 %copy-start.9 = (bf16[4,64,640]{2,1,0:T(8,128)(2,1)S(1)}, bf16[4,64,640]{2,1,0:T(8,128)(2,1)}, u32[]{:S(2)}) copy-start(bf16[4,64,640]{2,1,0:T(8,128)(2,1)} %copy-done.8) | copy-start | bytes 983044
  85.8 33.5 %collective-permute-start = (bf16[4,64,640]{2,1,0:T(8,128)(2,1)S(1)}, bf16[4,64,640]{2,1,0:T(8,128)(2,1)S(1)}, u32[]{:S(2)}, u32[]{:S(2)}) collective-permute-start(bf16[4,64,640]{2,1,0:T(8,128)(2,1)S(1)} %get-tuple-element.16), channel_id=1, source_target_pairs={{0,128},{1,129},{2,130},{3,131},{32,160},{33,161},{34,162},{35,163... | collective-permute-start | bytes 983048 | tf_op jit(solution)/shard_map/ppermute | solution.py:227
  88.9 30.4 %collective-permute-start.1 = (bf16[4,64,640]{2,1,0:T(8,128)(2,1)S(1)}, bf16[4,64,640]{2,1,0:T(8,128)(2,1)S(1)}, u32[]{:S(2)}, u32[]{:S(2)}) collective-permute-start(bf16[4,64,640]{2,1,0:T(8,128)(2,1)S(1)} %get-tuple-element.17), channel_id=1, source_target_pairs={{0,129},{1,130},{2,131},{3,160},{32,161},{33,162},{34,163},{35,192... | collective-permute-start | bytes 983048 | tf_op jit(solution)/shard_map/ppermute | solution.py:227
  95.3 24.0 %collective-permute-start.2 = (bf16[4,64,640]{2,1,0:T(8,128)(2,1)S(1)}, bf16[4,64,640]{2,1,0:T(8,128)(2,1)S(1)}, u32[]{:S(2)}, u32[]{:S(2)}) collective-permute-start(bf16[4,64,640]{2,1,0:T(8,128)(2,1)S(1)} %get-tuple-element.18), channel_id=1, source_target_pairs={{0,130},{1,227},{2,160},{3,129},{32,162},{33,131},{34,192},{35,161... | collective-permute-start | bytes 983048 | tf_op jit(solution)/shard_map/ppermute | solution.py:227
  97.8 21.5 %collective-permute-start.3 = (bf16[4,64,640]{2,1,0:T(8,128)(2,1)S(1)}, bf16[4,64,640]{2,1,0:T(8,128)(2,1)S(1)}, u32[]{:S(2)}, u32[]{:S(2)}) collective-permute-start(bf16[4,64,640]{2,1,0:T(8,128)(2,1)S(1)} %get-tuple-element.19), channel_id=1, source_target_pairs={{0,227},{1,128},{2,129},{3,130},{32,131},{33,160},{34,161},{35,162... | collective-permute-start | bytes 983048 | tf_op jit(solution)/shard_map/ppermute | solution.py:227
  120.8 21.3 %collective-permute-start.7 = (bf16[64,1024]{1,0:T(8,128)(2,1)}, bf16[64,1024]{1,0:T(8,128)(2,1)S(1)}, u32[]{:S(2)}, u32[]{:S(2)}) collective-permute-start(bf16[64,1024]{1,0:T(8,128)(2,1)} %get-tuple-element.22), channel_id=1, source_target_pairs={{0,32},{32,64},{64,96},{96,0},{1,33},{33,65},{65,97},{97,1},{2,34}... | collective-permute-start | bytes 393224 | tf_op jit(solution)/shard_map/ppermute | solution.py:208
  125.1 25.6 %collective-permute-start.8 = (bf16[64,1024]{1,0:T(8,128)(2,1)}, bf16[64,1024]{1,0:T(8,128)(2,1)S(1)}, u32[]{:S(2)}, u32[]{:S(2)}) collective-permute-start(bf16[64,1024]{1,0:T(8,128)(2,1)} %get-tuple-element.23), channel_id=1, source_target_pairs={{0,64},{32,96},{64,0},{96,32},{1,65},{33,97},{65,1},{97,33},{2,66}... | collective-permute-start | bytes 393224 | tf_op jit(solution)/shard_map/ppermute | solution.py:208
  132.4 29.4 %collective-permute-start.9 = (bf16[64,1024]{1,0:T(8,128)(2,1)}, bf16[64,1024]{1,0:T(8,128)(2,1)}, u32[]{:S(2)}, u32[]{:S(2)}) collective-permute-start(bf16[64,1024]{1,0:T(8,128)(2,1)} %get-tuple-element.24), channel_id=1, source_target_pairs={{0,96},{32,0},{64,32},{96,64},{1,97},{33,1},{65,33},{97,65},{2,98}... | collective-permute-start | bytes 393224 | tf_op jit(solution)/shard_map/ppermute | solution.py:208
  136.7 2.1 %copy-start.1 = (bf16[1,3,256,2560]{3,2,1,0:T(8,128)(2,1)S(1)}, bf16[1,3,256,2560]{3,2,1,0:T(8,128)(2,1)}, u32[]{:S(2)}) copy-start(bf16[1,3,256,2560]{3,2,1,0:T(8,128)(2,1)} %param.12) | copy-start | bytes 11796484
  (6 other events, 4.7 us)

commit v2 on v1

v2 whole, which is shorter than its diff:
```python
import functools

import jax
import jax.numpy as jnp
from jax import lax
from jax.experimental import pallas as pl
from jax.experimental.pallas import tpu as pltpu
from jax.sharding import Mesh, PartitionSpec as P

BF, F32 = jnp.bfloat16, jnp.float32
ZHI, YS, CORES, QS = 4, 4, 2, 4
DESTS = YS * CORES
HERE, MOST, TOK, TOP = 3, 6, 64, 6
SLOTS = ZHI * MOST
COLS = DESTS * HERE
ROWS = COLS * SLOTS
FEAT, HID = 640, 256
HSQ, WCOL = 384, 80
TALL = ZHI * TOK
XPAD = 32
BLOCKS = HERE * QS + 2
SEND = FEAT + HSQ
VM = pl.BlockSpec(memory_space=pltpu.VMEM)


def call(body, outs, args, flops=0, name=None, vmem=8):
    out_shape = [jax.ShapeDtypeStruct(s, t) for s, t in outs]
    size = sum(a.size * a.dtype.itemsize for a in (*args, *out_shape))
    return pl.pallas_call(
        body,
        out_shape=out_shape,
        in_specs=[VM] * len(args),
        out_specs=[VM] * len(outs),
        cost_estimate=pl.CostEstimate(flops=flops, bytes_accessed=size, transcendentals=0),
        compiler_params=pltpu.CompilerParams(vmem_limit_bytes=vmem * 2**20),
        name=name,
    )(*args)


def iota(shape, dim):
    return lax.broadcasted_iota(jnp.int32, shape, dim)


def dot(a, b, dims=((1,), (0,))):
    return lax.dot_general(a, b, (dims, ((), ())), preferred_element_type=F32)


def split_row(r):
    x = (r * 2731) >> 16
    rest = r - x * SLOTS
    group = (rest * 43) >> 8
    return x, group, rest - group * MOST


def fore_kernel(
    hidden, weight, columns, routes, gates, back_routes, back_gates, cot, shared,
    out, packed, held, ready, meta_ref, weight_sems, out_sems,
):
    loads = [
        pltpu.make_async_copy(weight.at[e], held.at[e], weight_sems.at[e]) for e in range(HERE)
    ]
    for load in loads:
        load.start()

    def leave(at, size, which):
        return pltpu.make_async_copy(
            ready.at[:, pl.ds(at, size)], out.at[:, pl.ds(at, size)], out_sems.at[which]
        )

    wide = columns[...].astype(F32)
    tiles = [wide[8 * m : 8 * m + 8, 128 * i : 128 * i + 128] for i in range(3) for m in range(10)]
    for b in range(2):
        lanes = [jnp.concatenate(tiles[3 * n : 3 * n + 3], axis=0) for n in range(5 * b, 5 * b + 5)]
        block = jnp.concatenate(lanes, axis=1).astype(BF)
        for d in range(DESTS):
            ready[d, BLOCKS - 2 + b] = block
    leaving = [leave(BLOCKS - 2, 2, HERE)]
    leaving[0].start()

    meta_ref[...] = jnp.zeros(meta_ref.shape, F32)
    for k in range(TOP):
        meta_ref[k : k + 1, 0:TOK] = routes[k].astype(F32)
        meta_ref[8 + k : 9 + k, 0:TOK] = back_routes[k].astype(F32)
        for at, gate in ((16, gates), (40, back_gates)):
            rest = gate[k]
            for i in range(3):
                part = rest.astype(BF).astype(F32)
                meta_ref[at + 8 * i + k : at + 8 * i + k + 1, 0:TOK] = part
                rest = rest - part
    packed[:, :FEAT] = cot[...]
    packed[:, FEAT:SEND] = shared[...]
    packed[:, SEND:] = meta_ref[...].T[:TOK, :].astype(BF)

    count = MOST * ZHI * DESTS
    to, src = iota((count, count), 0), iota((count, count), 1)
    slot, group = src >> 5, src & 31
    zhi, dest = group >> 3, group & 7
    perm = jnp.where(to == (dest * SLOTS + zhi * MOST + slot), 1.0, 0.0).astype(BF)
    for e in range(HERE):
        rows = dot(perm, hidden[e].reshape(count, HID)).astype(BF)
        loads[e].wait()
        for q in range(QS):
            value = dot(rows, held[e, :, q * FEAT : (q + 1) * FEAT])
            ready[:, e * QS + q] = value.reshape(DESTS, SLOTS, FEAT).astype(BF)
        leaving.append(leave(e * QS, QS, e))
        leaving[-1].start()
    for copy in leaving:
        copy.wait()


def back_kernel(rows, weight, out, got, held, row_sems, weight_sems):
    loads = []
    for e in range(HERE):
        loads.append(pltpu.make_async_copy(rows.at[:, e], got.at[e], row_sems.at[e]))
        loads.append(pltpu.make_async_copy(weight.at[e], held.at[e], weight_sems.at[e]))
    for load in loads:
        load.start()
    count = MOST * ZHI * DESTS
    to, src = iota((count, count), 0), iota((count, count), 1)
    slot, group = to >> 5, to & 31
    zhi, dest = group >> 3, group & 7
    perm = jnp.where(src == (dest * SLOTS + zhi * MOST + slot), 1.0, 0.0).astype(BF)
    for e in range(HERE):
        loads[2 * e].wait()
        loads[2 * e + 1].wait()
        total = jnp.zeros((count, HID), F32)
        for q in range(QS):
            piece = got[e, :, q].astype(F32).reshape(count, FEAT).astype(BF)
            total += dot(piece, held[e, :, q * FEAT : (q + 1) * FEAT], ((1,), (1,)))
        value = dot(perm, total.astype(BF)).astype(BF)
        out[e] = value.reshape(MOST, ZHI * DESTS, HID)


def unpacked_columns(rows):
    pieces = []
    for d in range(DESTS):
        blocks = [rows[d, BLOCKS - 2 + b].astype(F32) for b in range(2)]
        tiles = [
            blocks[n // 5][8 * m : 8 * m + 8, 128 * (n % 5) : 128 * (n % 5) + 128]
            for n in range(10)
            for m in range(3)
        ]
        lanes = [jnp.concatenate(tiles[10 * i : 10 * i + 10], axis=0) for i in range(3)]
        pieces.append(jnp.concatenate(lanes, axis=1))
    return jnp.concatenate(pieces, axis=0).astype(BF)


def select_kernel(whole, columns, cot0, cot1, cot2, cot3, out, grads):
    q = lax.axis_index("tensor")
    me = lax.axis_index("zhi")
    meta = whole[:, :, SEND:].astype(F32).reshape(TALL, 128).T
    names = iota((XPAD, TALL), 0) + me * COLS
    hit = jnp.zeros((XPAD, TALL), F32)
    gates = [jnp.zeros((XPAD, TALL), F32) for _ in range(3)]
    for k in range(TOP):
        found = jnp.where(meta[8 + k : 9 + k, :].astype(jnp.int32) == names, 1.0, 0.0)
        hit += found
        for i in range(3):
            gates[i] += found * meta[40 + 8 * i + k : 41 + 8 * i + k, :]
    a, b = iota((TALL, TALL), 0), iota((TALL, TALL), 1)
    before = jnp.where((a < b) & ((a >> 6) == (b >> 6)), 1.0, 0.0).astype(BF)
    slot = jnp.where(hit > 0, dot(hit.astype(BF), before), 100.0)
    x, _, _ = split_row(iota((ROWS, XPAD), 0))
    spread = jnp.where(x == iota((ROWS, XPAD), 1), 1.0, 0.0).astype(BF)
    slots = dot(spread, slot.astype(BF))
    gate = sum(dot(spread, g.astype(BF)) for g in gates)
    _, group, want = split_row(iota((ROWS, TALL), 0))
    chosen = (slots == want.astype(F32)) & (group == (iota((ROWS, TALL), 1) >> 6))
    pick = jnp.where(chosen, 1.0, 0.0).astype(BF)
    scale = jnp.sum(jnp.where(chosen, gate, 0.0), axis=1, keepdims=True)
    for i, cot in enumerate((cot0, cot1, cot2, cot3)):
        at = lax.rem(q + i, QS)
        here = cot[...].reshape(TALL, FEAT)
        value = dot(pick, here) * scale
        out[:, :, at] = value.reshape(DESTS, HERE, SLOTS, FEAT).astype(BF)

        @pl.when(at == me)
        def _(here=here):
            grads[...] = dot(here, columns[...]).reshape(ZHI, TOK, HSQ)


def combine_kernel(whole, rows, own, send1, send2, send3, columns):
    me = lax.axis_index("zhi")
    q = lax.axis_index("tensor")
    meta = whole[:, :, SEND:].astype(F32).reshape(TALL, 128)
    names = iota((TALL, 128), 1) + me * COLS
    hit = jnp.zeros((TALL, 128), F32)
    gates = [jnp.zeros((TALL, 128), F32) for _ in range(3)]
    for k in range(TOP):
        found = jnp.where(meta[:, k : k + 1].astype(jnp.int32) == names, 1.0, 0.0)
        hit += found
        for i in range(3):
            gates[i] += found * meta[:, 16 + 8 * i + k : 17 + 8 * i + k]
    a, b = iota((TALL, TALL), 0), iota((TALL, TALL), 1)
    before = jnp.where((b < a) & ((a >> 6) == (b >> 6)), 1.0, 0.0).astype(BF)
    slot = jnp.where(hit > 0, dot(before, hit.astype(BF)), 100.0)
    x, _, _ = split_row(iota((128, ROWS), 1))
    spread = jnp.where(x == iota((128, ROWS), 0), 1.0, 0.0).astype(BF)
    slots = dot(slot.astype(BF), spread)
    _, group, want = split_row(iota((TALL, ROWS), 1))
    chosen = (slots == want.astype(F32)) & (group == (iota((TALL, ROWS), 0) >> 6))
    mix = [jnp.where(chosen, dot(g.astype(BF), spread), 0.0).astype(BF) for g in gates]
    mix = jnp.concatenate(mix, axis=0)
    mine = unpacked_columns(rows)
    columns[...] = mine
    hidden = whole[:, :, FEAT:SEND].reshape(TALL, HSQ)
    shared = dot(hidden, mine, ((1,), (1,)))
    for i, out in enumerate((own, send1, send2, send3)):
        at = lax.rem(q + i, QS)
        piece = jnp.concatenate(
            [
                rows[d, e * QS + at].astype(F32)
                for d in range(DESTS)
                for e in range(HERE)
            ],
            axis=0,
        ).astype(BF)
        value = dot(mix, piece)
        value = value[:TALL] + value[TALL : 2 * TALL] + value[2 * TALL :]
        value += jnp.where(at == me, shared, 0.0)
        out[...] = value.reshape(ZHI, TOK, FEAT).astype(out.dtype)


def zsum_kernel(got0, got1, got2, got3, grads, own, *outs):
    me = lax.axis_index("zhi")
    for k in range(ZHI):
        at = lax.rem(me + k, ZHI)
        value = sum(got[at].astype(F32) for got in (got0, got1, got2, got3))
        out = own if k == 0 else outs[k - 1]
        out[:, :FEAT] = value.astype(out.dtype)
        out[:, FEAT:] = grads[at].astype(out.dtype)


def last_kernel(own, got1, got2, got3, layer, grad):
    value = own[...] + got1[...].astype(F32) + got2[...].astype(F32) + got3[...].astype(F32)
    layer[...] = value[:, :FEAT].astype(BF)
    grad[...] = value[:, FEAT:].astype(BF)


def moved(value, axes, count, step):
    return lax.ppermute(value, axes, [(i, (i + step) % count) for i in range(count)])


def z_pairs(step):
    total = ZHI * QS
    if step == 2:
        return [(z, (z + (2 if z % 2 == 0 else -2)) % total) for z in range(total)]
    return [(z, (z + step) % total) for z in range(total)]


def over_z(value, step):
    return lax.ppermute(value, ("zhi", "tensor"), z_pairs(step))


def on_device(
    forward_routes,
    forward_gates,
    hidden_rows,
    down_weight,
    shared_hidden,
    shared_weight,
    backward_routes,
    backward_gates,
    cotangent,
):
    weight = down_weight[0]
    hidden = jnp.transpose(hidden_rows[0], (0, 2, 1, 3))
    small = [
        jnp.transpose(a, (2, 0, 1))
        for a in (forward_routes, forward_gates, backward_routes, backward_gates)
    ]
    anywhere = pl.BlockSpec(memory_space=pl.ANY)
    product = 2 * HERE * 192 * HID * FEAT * QS
    parts, packed = pl.pallas_call(
        fore_kernel,
        in_specs=[VM, anywhere] + [VM] * 7,
        out_specs=[anywhere, VM],
        out_shape=[
            jax.ShapeDtypeStruct((DESTS, BLOCKS, SLOTS, FEAT), BF),
            jax.ShapeDtypeStruct((TOK, SEND + 128), BF),
        ],
        scratch_shapes=[
            pltpu.VMEM((HERE, HID, QS * FEAT), BF),
            pltpu.VMEM((DESTS, BLOCKS, SLOTS, FEAT), BF),
            pltpu.VMEM((128, 128), F32),
            pltpu.SemaphoreType.DMA((HERE,)),
            pltpu.SemaphoreType.DMA((HERE + 1,)),
        ],
        cost_estimate=pl.CostEstimate(flops=product, bytes_accessed=8 * 10**6, transcendentals=0),
        compiler_params=pltpu.CompilerParams(vmem_limit_bytes=58 * 2**20),
        name="expert_rows",
    )(hidden, weight, shared_weight[0].T, *small, cotangent[0], shared_hidden[0])
    arrived = lax.all_to_all(parts, ("y", "core"), 0, 0, tiled=True)

    whole = lax.all_gather(packed, "zhi", axis=0, tiled=False)
    held = whole[:, :, :FEAT]
    chunks = [held, over_z(held, -1), over_z(held, 2), over_z(held, 1)]

    chunk = ((ZHI, TOK, FEAT), BF)
    own, *sends, columns = call(
        combine_kernel,
        [((ZHI, TOK, FEAT), F32), chunk, chunk, chunk, ((FEAT, HSQ), BF)],
        [whole, arrived],
        flops=6 * TALL * ROWS * FEAT * QS,
        name="combine",
        vmem=14,
    )
    got = [over_z(value, step) for value, step in zip(sends, (1, 2, -1))]

    outgoing, grads = call(
        select_kernel,
        [((DESTS, HERE, QS, SLOTS, FEAT), BF), ((ZHI, TOK, HSQ), F32)],
        [whole, columns, *chunks],
        flops=2 * ROWS * TALL * FEAT * QS,
        name="select_rows",
        vmem=14,
    )
    outgoing, *got = lax.optimization_barrier((outgoing, *got))
    received = lax.all_to_all(outgoing, ("y", "core"), 0, 0, tiled=True)

    own, *sums = call(
        zsum_kernel,
        [((TOK, SEND), F32)] + [((TOK, SEND), BF)] * 3,
        [own, *got, grads],
        name="z_sum",
    )
    last = [moved(value, "zhi", ZHI, k) for k, value in zip((1, 2, 3), sums)]
    hidden_back = pl.pallas_call(
        back_kernel,
        in_specs=[anywhere, anywhere],
        out_specs=VM,
        out_shape=jax.ShapeDtypeStruct((HERE, MOST, ZHI * DESTS, HID), BF),
        scratch_shapes=[
            pltpu.VMEM((HERE, DESTS, QS, SLOTS, FEAT), BF),
            pltpu.VMEM((HERE, HID, QS * FEAT), BF),
            pltpu.SemaphoreType.DMA((HERE,)),
            pltpu.SemaphoreType.DMA((HERE,)),
        ],
        cost_estimate=pl.CostEstimate(flops=product, bytes_accessed=7 * 10**6, transcendentals=0),
        compiler_params=pltpu.CompilerParams(vmem_limit_bytes=58 * 2**20),
        name="hidden_back",
    )(received, weight)
    own, hidden_back = lax.optimization_barrier((own, hidden_back))
    layer, shared_back = call(
        last_kernel, [((TOK, FEAT), BF), ((TOK, HSQ), BF)], [own, *last], name="last_sum"
    )
    handed = moved(layer, "phase", 4, 1)

    return (
        handed[None],
        jnp.transpose(hidden_back, (0, 2, 1, 3))[None],
        shared_back[None],
    )


def solution(mesh):
    inner = Mesh(
        mesh.devices.reshape(4, ZHI, YS, CORES, QS), ("phase", "zhi", "y", "core", "tensor")
    )
    expert = ("zhi", "y", "core")
    return jax.shard_map(
        on_device,
        mesh=inner,
        in_specs=(
            P("phase", expert, None),
            P("phase", expert, None),
            P("phase", expert, None, None, "tensor"),
            P("phase", expert, "tensor", None),
            P("phase", expert, "tensor"),
            P("phase", "tensor", expert),
            P("phase", expert, None),
            P("phase", expert, None),
            P("phase", expert, "tensor"),
        ),
        out_specs=(
            P("phase", expert, "tensor"),
            P("phase", expert, None, None, "tensor"),
            P("phase", expert, "tensor"),
        ),
        check_vma=False,
    )
```

time: 164 us -> 143 us (0.87)
  the two profiles are of different devices: /device:TPU:65 before, /device:TPU:1 now
where the time goes in v2:
time: 143 us
  starting transfers between devices  59.2 us (41%)
  waiting for transfers between devices  28.8 us (20%)
  blocking collectives  28.5 us (20%)
  Pallas kernels  22.1 us (15%)
  local copies, waits for them, and re-layouts  3.39 us (2%)
    all_gather x1, blocking collectives, on_device(): whole = lax.all_gather(packed, 'zhi', axis=0, tiled=False)  28.5 us
    ppermute x6, starting transfers between devices, over_z(): return lax.ppermute(value, ('zhi', 'tensor'), z_pairs(step))  21.7 us
    ppermute x4, starting transfers between devices, moved(): lax.ppermute(value, axes, [(i, (i + step) % count) for i in range(count)])  21.2 us
    all_to_all x1, waiting for transfers between devices, on_device(): received = lax.all_to_all(outgoing, ('y', 'core'), 0, 0, tiled=True)  17.3 us
    pallas_call x4, Pallas kernels, call(): pl.pallas_call(body, out_shape=out_shape, in_specs=[VM] * len(args), out_...  11 us
    all_to_all x1, starting transfers between devices, on_device(): arrived = lax.all_to_all(parts, ('y', 'core'), 0, 0, tiled=True)  10.5 us
    ppermute x6, waiting for transfers between devices, over_z(): return lax.ppermute(value, ('zhi', 'tensor'), z_pairs(step))  6.11 us
    all_to_all x1, starting transfers between devices, on_device(): received = lax.all_to_all(outgoing, ('y', 'core'), 0, 0, tiled=True)  5.85 us
  transfers between devices with their start and end apart: 12, of which 5 were waited for; matrix products, arithmetic and copies ran while one was open for 1% of the time, Pallas kernels for 11%

profile of v2, /device:TPU:1, one launch (start us, length us, event | category | flops | bytes accessed | tf_op | source)
XLA Modules:
  0.0 142.7 jit_solution(5661167802133017723)
XLA Ops:
  0.6 5.8 %expert_rows.1 = (bf16[8,14,24,640]{3,2,1,0:T(8,128)(2,1)}, bf16[64,1152]{1,0:T(8,128)(2,1)}) custom-call(bf16[3,6,32,256]{3,2,1,0:T(8,128)(2,1)} %bitcast.25, bf16[3,256,2560]{2,1,0:T(8,128)(2,1)} %bitcast.22, bf16[80,384]{1,0:T(8,128)(2,1)} %bitcast.28, s32[6,1,64]{2,1,0:T(1,128)} %bitcast.30, f32[6,1,64]{2,1,0:T(1,128)} %bitcast.31, ...), custom_call_target="tpu_custom_call" | custom-call | flops 754974720 | bytes 8000000 | tf_op jit(solution)/shard_map/expert_rows/pallas_call | solution.py:274
  6.4 10.5 %all-to-all-start = ((bf16[8,14,24,640]{3,2,1,0:T(8,128)(2,1)}), bf16[8,14,24,640]{3,2,1,0:T(8,128)(2,1)S(1)}, u32[]{:S(2)}, u32[]{:S(2)}) async-start(bf16[8,14,24,640]{3,2,1,0:T(8,128)(2,1)} %get-tuple-element.25), calls=%async_computation | async-start | bytes 6881280 | tf_op jit(solution)/shard_map/all_to_all | solution.py:293
  16.9 28.5 %all-gather = bf16[256,1152]{1,0:T(8,128)(2,1)S(1)} all-gather(bf16[64,1152]{1,0:T(8,128)(2,1)} %get-tuple-element.24), channel_id=2, replica_groups=mesh['phase'=4,'zhi'=4,'y'=4,'core'=2,'tensor'=4] {'zhi'}, dimensions={0}, use_global_device_ids=true | all-gather | bytes 737280 | tf_op jit(solution)/shard_map/all_gather | solution.py:295
  46.2 1.9 %collective-permute-start.2 = (bf16[4,64,640]{2,1,0:T(8,128)(2,1)}, bf16[4,64,640]{2,1,0:T(8,128)(2,1)}, u32[]{:S(2)}, u32[]{:S(2)}) collective-permute-start(bf16[4,64,640]{2,1,0:T(8,128)(2,1)} %slice.4.cot0), channel_id=1, source_target_pairs={{0,1},{1,2},{2,3},{3,32},{32,33},{33,34},{34,35},{35,64},{64,65},{... | collective-permute-start | bytes 983048 | tf_op jit(solution)/shard_map/ppermute | solution.py:252
  48.1 4.2 %collective-permute-start.1 = (bf16[4,64,640]{2,1,0:T(8,128)(2,1)}, bf16[4,64,640]{2,1,0:T(8,128)(2,1)}, u32[]{:S(2)}, u32[]{:S(2)}) collective-permute-start(bf16[4,64,640]{2,1,0:T(8,128)(2,1)} %slice.4.cot0), channel_id=1, source_target_pairs={{0,2},{1,99},{2,32},{3,1},{32,34},{33,3},{34,64},{35,33},{64,66},{... | collective-permute-start | bytes 983048 | tf_op jit(solution)/shard_map/ppermute | solution.py:252
  52.3 3.2 %collective-permute-start = (bf16[4,64,640]{2,1,0:T(8,128)(2,1)}, bf16[4,64,640]{2,1,0:T(8,128)(2,1)}, u32[]{:S(2)}, u32[]{:S(2)}) collective-permute-start(bf16[4,64,640]{2,1,0:T(8,128)(2,1)} %slice.4.cot0), channel_id=1, source_target_pairs={{0,99},{1,0},{2,1},{3,2},{32,3},{33,32},{34,33},{35,34},{64,35},{6... | collective-permute-start | bytes 983048 | tf_op jit(solution)/shard_map/ppermute | solution.py:252
  55.6 2.1 %all-to-all-done.rows = bf16[8,14,24,640]{3,2,1,0:T(8,128)(2,1)S(1)} async-done(((bf16[8,14,24,640]{3,2,1,0:T(8,128)(2,1)}), bf16[8,14,24,640]{3,2,1,0:T(8,128)(2,1)S(1)}, u32[]{:S(2)}, u32[]{:S(2)}) %all-to-all-start) | async-done | bytes 3440672 | tf_op jit(solution)/shard_map/all_to_all | solution.py:293
  57.6 1.1 copy-done.1
  58.7 4.8 %combine.1 = (f32[4,64,640]{2,1,0:T(8,128)S(1)}, bf16[4,64,640]{2,1,0:T(8,128)(2,1)S(1)}, bf16[4,64,640]{2,1,0:T(8,128)(2,1)S(1)}, bf16[4,64,640]{2,1,0:T(8,128)(2,1)S(1)}, bf16[640,384]{1,0:T(8,128)(2,1)S(1)}) custom-call(bf16[4,64,1152]{2,1,0:T(8,128)(2,1)S(1)} %bitcast.20, bf16[8,14,24,640]{3,2,1,0:T(8,128)(2,1)S(1)} %all-to-all-done.rows), custom_call_target="tpu_custom_call" | custom-call | flops 2264924160 | bytes 6160384 | tf_op jit(solution)/shard_map/combine/pallas_call | solution.py:29
  63.5 0.8 copy-done.2
  64.4 1.9 %collective-permute-start.3 = (bf16[4,64,640]{2,1,0:T(8,128)(2,1)S(1)}, bf16[4,64,640]{2,1,0:T(8,128)(2,1)S(1)}, u32[]{:S(2)}, u32[]{:S(2)}) collective-permute-start(bf16[4,64,640]{2,1,0:T(8,128)(2,1)S(1)} %get-tuple-element.29), channel_id=1, source_target_pairs={{0,1},{1,2},{2,3},{3,32},{32,33},{33,34},{34,35},{35,64},{64,65},{... | collective-permute-start | bytes 983048 | tf_op jit(solution)/shard_map/ppermute | solution.py:252
  66.3 2.0 %collective-permute-start.4 = (bf16[4,64,640]{2,1,0:T(8,128)(2,1)S(1)}, bf16[4,64,640]{2,1,0:T(8,128)(2,1)S(1)}, u32[]{:S(2)}, u32[]{:S(2)}) collective-permute-start(bf16[4,64,640]{2,1,0:T(8,128)(2,1)S(1)} %get-tuple-element.30), channel_id=1, source_target_pairs={{0,2},{1,99},{2,32},{3,1},{32,34},{33,3},{34,64},{35,33},{64,66},{... | collective-permute-start | bytes 983048 | tf_op jit(solution)/shard_map/ppermute | solution.py:252
  68.4 8.4 %collective-permute-start.5 = (bf16[4,64,640]{2,1,0:T(8,128)(2,1)S(1)}, bf16[4,64,640]{2,1,0:T(8,128)(2,1)S(1)}, u32[]{:S(2)}, u32[]{:S(2)}) collective-permute-start(bf16[4,64,640]{2,1,0:T(8,128)(2,1)S(1)} %get-tuple-element.31), channel_id=1, source_target_pairs={{0,99},{1,0},{2,1},{3,2},{32,3},{33,32},{34,33},{35,34},{64,35},{6... | collective-permute-start | bytes 983048 | tf_op jit(solution)/shard_map/ppermute | solution.py:252
  76.8 5.4 %select_rows.1 = (bf16[8,3,4,24,640]{4,3,2,1,0:T(8,128)(2,1)}, f32[4,64,384]{2,1,0:T(8,128)S(1)}) custom-call(bf16[4,64,1152]{2,1,0:T(8,128)(2,1)S(1)} %bitcast.21, bf16[640,384]{1,0:T(8,128)(2,1)S(1)} %get-tuple-element.27.columns, bf16[4,64,640]{2,1,0:T(8,128)(2,1)} %slice.4.cot0, bf16[4,64,640]{2,1,0:T(8,128)(2,1)} %collective-permute-done.cot1, ...), custom_call_target="tpu_custom_call" | custom-call | flops 754974720 | bytes 5734400 | tf_op jit(solution)/shard_map/select_rows/pallas_call | solution.py:29
  82.2 3.9 %collective-permute-done.4.got2 = bf16[4,64,640]{2,1,0:T(8,128)(2,1)S(1)} collective-permute-done((bf16[4,64,640]{2,1,0:T(8,128)(2,1)S(1)}, bf16[4,64,640]{2,1,0:T(8,128)(2,1)S(1)}, u32[]{:S(2)}, u32[]{:S(2)}) %collective-permute-start.4) | collective-permute-done | bytes 327712 | tf_op jit(solution)/shard_map/ppermute | solution.py:252
  86.1 2.2 %collective-permute-done.5.got3 = bf16[4,64,640]{2,1,0:T(8,128)(2,1)S(1)} collective-permute-done((bf16[4,64,640]{2,1,0:T(8,128)(2,1)S(1)}, bf16[4,64,640]{2,1,0:T(8,128)(2,1)S(1)}, u32[]{:S(2)}, u32[]{:S(2)}) %collective-permute-start.5) | collective-permute-done | bytes 327712 | tf_op jit(solution)/shard_map/ppermute | solution.py:252
  88.3 5.9 %all-to-all-start.1 = ((bf16[8,3,4,24,640]{4,3,2,1,0:T(8,128)(2,1)}), bf16[8,3,4,24,640]{4,3,2,1,0:T(8,128)(2,1)}, u32[]{:S(2)}, u32[]{:S(2)}) async-start(bf16[8,3,4,24,640]{4,3,2,1,0:T(8,128)(2,1)} %get-tuple-element.37), calls=%async_computation.1 | async-start | bytes 5898240 | tf_op jit(solution)/shard_map/all_to_all | solution.py:319
  94.3 2.2 %collective-permute-start.6 = (bf16[64,1024]{1,0:T(8,128)(2,1)S(1)}, bf16[64,1024]{1,0:T(8,128)(2,1)S(1)}, u32[]{:S(2)}, u32[]{:S(2)}) collective-permute-start(bf16[64,1024]{1,0:T(8,128)(2,1)S(1)} %get-tuple-element.39), channel_id=1, source_target_pairs={{0,32},{32,64},{64,96},{96,0},{1,33},{33,65},{65,97},{97,1},{2,34}... | collective-permute-start | bytes 393224 | tf_op jit(solution)/shard_map/ppermute | solution.py:241
  96.5 10.7 %collective-permute-start.7 = (bf16[64,1024]{1,0:T(8,128)(2,1)S(1)}, bf16[64,1024]{1,0:T(8,128)(2,1)S(1)}, u32[]{:S(2)}, u32[]{:S(2)}) collective-permute-start(bf16[64,1024]{1,0:T(8,128)(2,1)S(1)} %get-tuple-element.40), channel_id=1, source_target_pairs={{0,64},{32,96},{64,0},{96,32},{1,65},{33,97},{65,1},{97,33},{2,66}... | collective-permute-start | bytes 393224 | tf_op jit(solution)/shard_map/ppermute | solution.py:241
  107.2 5.2 %collective-permute-start.8 = (bf16[64,1024]{1,0:T(8,128)(2,1)S(1)}, bf16[64,1024]{1,0:T(8,128)(2,1)S(1)}, u32[]{:S(2)}, u32[]{:S(2)}) collective-permute-start(bf16[64,1024]{1,0:T(8,128)(2,1)S(1)} %get-tuple-element.41), channel_id=1, source_target_pairs={{0,96},{32,0},{64,32},{96,64},{1,97},{33,1},{65,33},{97,65},{2,98}... | collective-permute-start | bytes 393224 | tf_op jit(solution)/shard_map/ppermute | solution.py:241
  112.4 17.3 %all-to-all-done.1.rows = bf16[8,3,4,24,640]{4,3,2,1,0:T(8,128)(2,1)} async-done(((bf16[8,3,4,24,640]{4,3,2,1,0:T(8,128)(2,1)}), bf16[8,3,4,24,640]{4,3,2,1,0:T(8,128)(2,1)}, u32[]{:S(2)}, u32[]{:S(2)}) %all-to-all-start.1) | async-done | bytes 2949152 | tf_op jit(solution)/shard_map/all_to_all | solution.py:319
  129.7 5.3 %hidden_back.1 = bf16[3,6,32,256]{3,2,1,0:T(8,128)(2,1)} custom-call(bf16[8,3,4,24,640]{4,3,2,1,0:T(8,128)(2,1)} %all-to-all-done.1.rows, bf16[3,256,2560]{2,1,0:T(8,128)(2,1)} %bitcast.23), custom_call_target="tpu_custom_call" | custom-call | flops 754974720 | bytes 7000000 | tf_op jit(solution)/shard_map/hidden_back/pallas_call | solution.py:328
  135.7 3.1 %collective-permute-start.9 = (bf16[64,640]{1,0:T(8,128)(2,1)S(1)}, bf16[64,640]{1,0:T(8,128)(2,1)S(1)}, u32[]{:S(2)}, u32[]{:S(2)}) collective-permute-start(bf16[64,640]{1,0:T(8,128)(2,1)S(1)} %get-tuple-element.42), channel_id=1, source_target_pairs={{0,128},{128,256},{256,384},{384,0},{1,129},{129,257},{257,385},{3... | collective-permute-start | bytes 245768 | tf_op jit(solution)/shard_map/ppermute | solution.py:241
  138.8 3.3 %collective-permute-done.9 = bf16[64,640]{1,0:T(8,128)(2,1)S(1)} collective-permute-done((bf16[64,640]{1,0:T(8,128)(2,1)S(1)}, bf16[64,640]{1,0:T(8,128)(2,1)S(1)}, u32[]{:S(2)}, u32[]{:S(2)}) %collective-permute-start.9) | collective-permute-done | bytes 81952 | tf_op jit(solution)/shard_map/ppermute | solution.py:241
  (17 shorter events, 2.3 us)
Async XLA Ops:
  6.4 51.2 %all-to-all-start = ((bf16[8,14,24,640]{3,2,1,0:T(8,128)(2,1)}), bf16[8,14,24,640]{3,2,1,0:T(8,128)(2,1)S(1)}, u32[]{:S(2)}, u32[]{:S(2)}) async-start(bf16[8,14,24,640]{3,2,1,0:T(8,128)(2,1)} %get-tuple-element.25), calls=%async_computation | async-start | bytes 6881280 | tf_op jit(solution)/shard_map/all_to_all | solution.py:293
  45.3 7.0 %copy-start = (bf16[256,1152]{1,0:T(8,128)(2,1)}, bf16[256,1152]{1,0:T(8,128)(2,1)S(1)}, u32[]{:S(2)}) copy-start(bf16[256,1152]{1,0:T(8,128)(2,1)S(1)} %all-gather) | copy-start | bytes 1769476
  46.2 22.2 %collective-permute-start.2 = (bf16[4,64,640]{2,1,0:T(8,128)(2,1)}, bf16[4,64,640]{2,1,0:T(8,128)(2,1)}, u32[]{:S(2)}, u32[]{:S(2)}) collective-permute-start(bf16[4,64,640]{2,1,0:T(8,128)(2,1)} %slice.4.cot0), channel_id=1, source_target_pairs={{0,1},{1,2},{2,3},{3,32},{32,33},{33,34},{34,35},{35,64},{64,65},{... | collective-permute-start | bytes 983048 | tf_op jit(solution)/shard_map/ppermute | solution.py:252
  48.1 28.7 %collective-permute-start.1 = (bf16[4,64,640]{2,1,0:T(8,128)(2,1)}, bf16[4,64,640]{2,1,0:T(8,128)(2,1)}, u32[]{:S(2)}, u32[]{:S(2)}) collective-permute-start(bf16[4,64,640]{2,1,0:T(8,128)(2,1)} %slice.4.cot0), channel_id=1, source_target_pairs={{0,2},{1,99},{2,32},{3,1},{32,34},{33,3},{34,64},{35,33},{64,66},{... | collective-permute-start | bytes 983048 | tf_op jit(solution)/shard_map/ppermute | solution.py:252
  52.3 24.5 %collective-permute-start = (bf16[4,64,640]{2,1,0:T(8,128)(2,1)}, bf16[4,64,640]{2,1,0:T(8,128)(2,1)}, u32[]{:S(2)}, u32[]{:S(2)}) collective-permute-start(bf16[4,64,640]{2,1,0:T(8,128)(2,1)} %slice.4.cot0), channel_id=1, source_target_pairs={{0,99},{1,0},{2,1},{3,2},{32,3},{33,32},{34,33},{35,34},{64,35},{6... | collective-permute-start | bytes 983048 | tf_op jit(solution)/shard_map/ppermute | solution.py:252
  57.6 1.1 copy-start.1
  63.5 0.9 copy-start.2
  64.4 17.8 %collective-permute-start.3 = (bf16[4,64,640]{2,1,0:T(8,128)(2,1)S(1)}, bf16[4,64,640]{2,1,0:T(8,128)(2,1)S(1)}, u32[]{:S(2)}, u32[]{:S(2)}) collective-permute-start(bf16[4,64,640]{2,1,0:T(8,128)(2,1)S(1)} %get-tuple-element.29), channel_id=1, source_target_pairs={{0,1},{1,2},{2,3},{3,32},{32,33},{33,34},{34,35},{35,64},{64,65},{... | collective-permute-start | bytes 983048 | tf_op jit(solution)/shard_map/ppermute | solution.py:252
  66.3 19.7 %collective-permute-start.4 = (bf16[4,64,640]{2,1,0:T(8,128)(2,1)S(1)}, bf16[4,64,640]{2,1,0:T(8,128)(2,1)S(1)}, u32[]{:S(2)}, u32[]{:S(2)}) collective-permute-start(bf16[4,64,640]{2,1,0:T(8,128)(2,1)S(1)} %get-tuple-element.30), channel_id=1, source_target_pairs={{0,2},{1,99},{2,32},{3,1},{32,34},{33,3},{34,64},{35,33},{64,66},{... | collective-permute-start | bytes 983048 | tf_op jit(solution)/shard_map/ppermute | solution.py:252
  68.4 19.9 %collective-permute-start.5 = (bf16[4,64,640]{2,1,0:T(8,128)(2,1)S(1)}, bf16[4,64,640]{2,1,0:T(8,128)(2,1)S(1)}, u32[]{:S(2)}, u32[]{:S(2)}) collective-permute-start(bf16[4,64,640]{2,1,0:T(8,128)(2,1)S(1)} %get-tuple-element.31), channel_id=1, source_target_pairs={{0,99},{1,0},{2,1},{3,2},{32,3},{33,32},{34,33},{35,34},{64,35},{6... | collective-permute-start | bytes 983048 | tf_op jit(solution)/shard_map/ppermute | solution.py:252
  82.2 12.0 %copy-start.3 = (f32[4,64,640]{2,1,0:T(8,128)S(1)}, f32[4,64,640]{2,1,0:T(8,128)}, u32[]{:S(2)}) copy-start(f32[4,64,640]{2,1,0:T(8,128)} %copy-done.2) | copy-start | bytes 1966084
  88.3 41.4 %all-to-all-start.1 = ((bf16[8,3,4,24,640]{4,3,2,1,0:T(8,128)(2,1)}), bf16[8,3,4,24,640]{4,3,2,1,0:T(8,128)(2,1)}, u32[]{:S(2)}, u32[]{:S(2)}) async-start(bf16[8,3,4,24,640]{4,3,2,1,0:T(8,128)(2,1)} %get-tuple-element.37), calls=%async_computation.1 | async-start | bytes 5898240 | tf_op jit(solution)/shard_map/all_to_all | solution.py:319
  94.3 40.8 %collective-permute-start.6 = (bf16[64,1024]{1,0:T(8,128)(2,1)S(1)}, bf16[64,1024]{1,0:T(8,128)(2,1)S(1)}, u32[]{:S(2)}, u32[]{:S(2)}) collective-permute-start(bf16[64,1024]{1,0:T(8,128)(2,1)S(1)} %get-tuple-element.39), channel_id=1, source_target_pairs={{0,32},{32,64},{64,96},{96,0},{1,33},{33,65},{65,97},{97,1},{2,34}... | collective-permute-start | bytes 393224 | tf_op jit(solution)/shard_map/ppermute | solution.py:241
  96.5 38.5 %collective-permute-start.7 = (bf16[64,1024]{1,0:T(8,128)(2,1)S(1)}, bf16[64,1024]{1,0:T(8,128)(2,1)S(1)}, u32[]{:S(2)}, u32[]{:S(2)}) collective-permute-start(bf16[64,1024]{1,0:T(8,128)(2,1)S(1)} %get-tuple-element.40), channel_id=1, source_target_pairs={{0,64},{32,96},{64,0},{96,32},{1,65},{33,97},{65,1},{97,33},{2,66}... | collective-permute-start | bytes 393224 | tf_op jit(solution)/shard_map/ppermute | solution.py:241
  107.2 27.9 %collective-permute-start.8 = (bf16[64,1024]{1,0:T(8,128)(2,1)S(1)}, bf16[64,1024]{1,0:T(8,128)(2,1)S(1)}, u32[]{:S(2)}, u32[]{:S(2)}) collective-permute-start(bf16[64,1024]{1,0:T(8,128)(2,1)S(1)} %get-tuple-element.41), channel_id=1, source_target_pairs={{0,96},{32,0},{64,32},{96,64},{1,97},{33,1},{65,33},{97,65},{2,98}... | collective-permute-start | bytes 393224 | tf_op jit(solution)/shard_map/ppermute | solution.py:241
  135.7 6.4 %collective-permute-start.9 = (bf16[64,640]{1,0:T(8,128)(2,1)S(1)}, bf16[64,640]{1,0:T(8,128)(2,1)S(1)}, u32[]{:S(2)}, u32[]{:S(2)}) collective-permute-start(bf16[64,640]{1,0:T(8,128)(2,1)S(1)} %get-tuple-element.42), channel_id=1, source_target_pairs={{0,128},{128,256},{256,384},{384,0},{1,129},{129,257},{257,385},{3... | collective-permute-start | bytes 245768 | tf_op jit(solution)/shard_map/ppermute | solution.py:241

commit v3 on v2

--- a/solution.py
+++ b/solution.py
@@ -221,20 +221,33 @@
         out[...] = value.reshape(ZHI, TOK, FEAT).astype(out.dtype)
 
 
-def zsum_kernel(got0, got1, got2, got3, grads, own, *outs):
+def zsum_kernel(got0, got1, got2, got3, grads, own, held, far, near):
     me = lax.axis_index("zhi")
-    for k in range(ZHI):
+    step = 1 + 2 * lax.axis_index("core")
+    for k, out in ((0, own), (step, held), (2, far), (ZHI - step, near)):
         at = lax.rem(me + k, ZHI)
         value = sum(got[at].astype(F32) for got in (got0, got1, got2, got3))
-        out = own if k == 0 else outs[k - 1]
         out[:, :FEAT] = value.astype(out.dtype)
         out[:, FEAT:] = grads[at].astype(out.dtype)
 
 
-def last_kernel(own, got1, got2, got3, layer, grad):
-    value = own[...] + got1[...].astype(F32) + got2[...].astype(F32) + got3[...].astype(F32)
+def relay_kernel(held, passing, out):
+    out[...] = (held[...] + passing[...].astype(F32)).astype(BF)
+
+
+def last_kernel(own, got1, got2, layer, grad):
+    value = own[...] + got1[...].astype(F32) + got2[...].astype(F32)
     layer[...] = value[:, :FEAT].astype(BF)
     grad[...] = value[:, FEAT:].astype(BF)
+
+
+def ahead(value, sign):
+    pairs = [
+        (z * CORES + c, (z + sign * (1 - 2 * c)) % ZHI * CORES + c)
+        for z in range(ZHI)
+        for c in range(CORES)
+    ]
+    return lax.ppermute(value, ("zhi", "core"), pairs)
 
 
 def moved(value, axes, count, step):
@@ -318,13 +331,21 @@
     outgoing, *got = lax.optimization_barrier((outgoing, *got))
     received = lax.all_to_all(outgoing, ("y", "core"), 0, 0, tiled=True)
 
-    own, *sums = call(
+    own, held, far, near = call(
         zsum_kernel,
-        [((TOK, SEND), F32)] + [((TOK, SEND), BF)] * 3,
+        [((TOK, SEND), F32), ((TOK, SEND), F32), ((TOK, SEND), BF), ((TOK, SEND), BF)],
         [own, *got, grads],
         name="z_sum",
     )
-    last = [moved(value, "zhi", ZHI, k) for k, value in zip((1, 2, 3), sums)]
+    passing, near = ahead(far, 1), ahead(near, -1)
+    [further] = call(relay_kernel, [((TOK, SEND), BF)], [held, passing], name="z_relay")
+    last = [near, ahead(further, 1)]
+    layer, shared_back = call(
+        last_kernel, [((TOK, FEAT), BF), ((TOK, HSQ), BF)], [own, *last], name="last_sum"
+    )
+    handed = moved(layer, "phase", 4, 1)
+
+    layer, received = lax.optimization_barrier((layer, received))
     hidden_back = pl.pallas_call(
         back_kernel,
         in_specs=[anywhere, anywhere],
@@ -340,12 +361,6 @@
         compiler_params=pltpu.CompilerParams(vmem_limit_bytes=58 * 2**20),
         name="hidden_back",
     )(received, weight)
-    own, hidden_back = lax.optimization_barrier((own, hidden_back))
-    layer, shared_back = call(
-        last_kernel, [((TOK, FEAT), BF), ((TOK, HSQ), BF)], [own, *last], name="last_sum"
-    )
-    handed = moved(layer, "phase", 4, 1)
-
     return (
         handed[None],
         jnp.transpose(hidden_back, (0, 2, 1, 3))[None],

time: 143 us -> 136 us (0.951)
  waiting for transfers between devices: 28.8 us -> 23.4 us
  starting transfers between devices: 59.2 us -> 57.5 us
    ppermute x4 -> x1, starting transfers between devices: 21.2 us -> 3.1 us  [moved(): lax.ppermute(value, axes, [(i, (i + step) % count) for i in range(count)])]
    ppermute x0 -> x3, starting transfers between devices: none -> 16.4 us  [ahead(): return lax.ppermute(value, ('zhi', 'core'), pairs)]
    all_to_all x1, waiting for transfers between devices: 17.3 us -> 2.92 us  [on_device(): received = lax.all_to_all(outgoing, ('y', 'core'), 0, 0, tiled=True)]
    ppermute x0 -> x3, waiting for transfers between devices: none -> 8.59 us  [ahead(): return lax.ppermute(value, ('zhi', 'core'), pairs)]
    ppermute x4 -> x1, waiting for transfers between devices: 3.27 us -> 3.67 us  [moved(): lax.ppermute(value, axes, [(i, (i + step) % count) for i in range(count)])]
    pallas_call x4 -> x5, Pallas kernels: 11 us -> 11 us  [call(): pl.pallas_call(body, out_shape=out_shape, in_specs=[VM] * len(args), out_...]
  transfers between devices with their start and end apart: 12 -> 12, of which waited for: 5 -> 8; matrix products, arithmetic and copies ran while one was open for 1% -> 1% of each run, Pallas kernels for 11% -> 8%
where the time goes in v3:
time: 136 us
  starting transfers between devices  57.5 us (42%)
  blocking collectives  28.5 us (21%)
  waiting for transfers between devices  23.4 us (17%)
  Pallas kernels  22.1 us (16%)
  local copies, waits for them, and re-layouts  3.39 us (2%)
    all_gather x1, blocking collectives, on_device(): whole = lax.all_gather(packed, 'zhi', axis=0, tiled=False)  28.5 us
    ppermute x6, starting transfers between devices, over_z(): return lax.ppermute(value, ('zhi', 'tensor'), z_pairs(step))  21.7 us
    ppermute x3, starting transfers between devices, ahead(): return lax.ppermute(value, ('zhi', 'core'), pairs)  16.4 us
    pallas_call x5, Pallas kernels, call(): pl.pallas_call(body, out_shape=out_shape, in_specs=[VM] * len(args), out_...  11 us
    all_to_all x1, starting transfers between devices, on_device(): arrived = lax.all_to_all(parts, ('y', 'core'), 0, 0, tiled=True)  10.5 us
    ppermute x3, waiting for transfers between devices, ahead(): return lax.ppermute(value, ('zhi', 'core'), pairs)  8.59 us
    ppermute x6, waiting for transfers between devices, over_z(): return lax.ppermute(value, ('zhi', 'tensor'), z_pairs(step))  6.11 us
    all_to_all x1, starting transfers between devices, on_device(): received = lax.all_to_all(outgoing, ('y', 'core'), 0, 0, tiled=True)  5.85 us
  transfers between devices with their start and end apart: 12, of which 8 were waited for; matrix products, arithmetic and copies ran while one was open for 1% of the time, Pallas kernels for 8%

profile of v3, /device:TPU:1, one launch (start us, length us, event | category | flops | bytes accessed | tf_op | source)
XLA Modules:
  0.0 135.7 jit_solution(7108787190144166720)
XLA Ops:
  0.6 5.8 %expert_rows.1 = (bf16[8,14,24,640]{3,2,1,0:T(8,128)(2,1)}, bf16[64,1152]{1,0:T(8,128)(2,1)}) custom-call(bf16[3,6,32,256]{3,2,1,0:T(8,128)(2,1)} %bitcast.25, bf16[3,256,2560]{2,1,0:T(8,128)(2,1)} %bitcast.22, bf16[80,384]{1,0:T(8,128)(2,1)} %bitcast.28, s32[6,1,64]{2,1,0:T(1,128)} %bitcast.30, f32[6,1,64]{2,1,0:T(1,128)} %bitcast.31, ...), custom_call_target="tpu_custom_call" | custom-call | flops 754974720 | bytes 8000000 | tf_op jit(solution)/shard_map/expert_rows/pallas_call | solution.py:287
  6.4 10.5 %all-to-all-start = ((bf16[8,14,24,640]{3,2,1,0:T(8,128)(2,1)}), bf16[8,14,24,640]{3,2,1,0:T(8,128)(2,1)S(1)}, u32[]{:S(2)}, u32[]{:S(2)}) async-start(bf16[8,14,24,640]{3,2,1,0:T(8,128)(2,1)} %get-tuple-element.24), calls=%async_computation | async-start | bytes 6881280 | tf_op jit(solution)/shard_map/all_to_all | solution.py:306
  16.9 28.5 %all-gather = bf16[256,1152]{1,0:T(8,128)(2,1)S(1)} all-gather(bf16[64,1152]{1,0:T(8,128)(2,1)} %get-tuple-element.23), channel_id=2, replica_groups=mesh['phase'=4,'zhi'=4,'y'=4,'core'=2,'tensor'=4] {'zhi'}, dimensions={0}, use_global_device_ids=true | all-gather | bytes 737280 | tf_op jit(solution)/shard_map/all_gather | solution.py:308
  46.2 1.9 %collective-permute-start.2 = (bf16[4,64,640]{2,1,0:T(8,128)(2,1)}, bf16[4,64,640]{2,1,0:T(8,128)(2,1)}, u32[]{:S(2)}, u32[]{:S(2)}) collective-permute-start(bf16[4,64,640]{2,1,0:T(8,128)(2,1)} %slice.4.cot0), channel_id=1, source_target_pairs={{0,1},{1,2},{2,3},{3,32},{32,33},{33,34},{34,35},{35,64},{64,65},{... | collective-permute-start | bytes 983048 | tf_op jit(solution)/shard_map/ppermute | solution.py:265
  48.1 4.2 %collective-permute-start.1 = (bf16[4,64,640]{2,1,0:T(8,128)(2,1)}, bf16[4,64,640]{2,1,0:T(8,128)(2,1)}, u32[]{:S(2)}, u32[]{:S(2)}) collective-permute-start(bf16[4,64,640]{2,1,0:T(8,128)(2,1)} %slice.4.cot0), channel_id=1, source_target_pairs={{0,2},{1,99},{2,32},{3,1},{32,34},{33,3},{34,64},{35,33},{64,66},{... | collective-permute-start | bytes 983048 | tf_op jit(solution)/shard_map/ppermute | solution.py:265
  52.3 3.2 %collective-permute-start = (bf16[4,64,640]{2,1,0:T(8,128)(2,1)}, bf16[4,64,640]{2,1,0:T(8,128)(2,1)}, u32[]{:S(2)}, u32[]{:S(2)}) collective-permute-start(bf16[4,64,640]{2,1,0:T(8,128)(2,1)} %slice.4.cot0), channel_id=1, source_target_pairs={{0,99},{1,0},{2,1},{3,2},{32,3},{33,32},{34,33},{35,34},{64,35},{6... | collective-permute-start | bytes 983048 | tf_op jit(solution)/shard_map/ppermute | solution.py:265
  55.6 2.1 %all-to-all-done.rows = bf16[8,14,24,640]{3,2,1,0:T(8,128)(2,1)S(1)} async-done(((bf16[8,14,24,640]{3,2,1,0:T(8,128)(2,1)}), bf16[8,14,24,640]{3,2,1,0:T(8,128)(2,1)S(1)}, u32[]{:S(2)}, u32[]{:S(2)}) %all-to-all-start) | async-done | bytes 3440672 | tf_op jit(solution)/shard_map/all_to_all | solution.py:306
  58.7 4.8 %combine.1 = (f32[4,64,640]{2,1,0:T(8,128)S(1)}, bf16[4,64,640]{2,1,0:T(8,128)(2,1)S(1)}, bf16[4,64,640]{2,1,0:T(8,128)(2,1)S(1)}, bf16[4,64,640]{2,1,0:T(8,128)(2,1)S(1)}, bf16[640,384]{1,0:T(8,128)(2,1)S(1)}) custom-call(bf16[4,64,1152]{2,1,0:T(8,128)(2,1)S(1)} %bitcast.20, bf16[8,14,24,640]{3,2,1,0:T(8,128)(2,1)S(1)} %all-to-all-done.rows), custom_call_target="tpu_custom_call" | custom-call | flops 2264924160 | bytes 6160384 | tf_op jit(solution)/shard_map/combine/pallas_call | solution.py:29
  64.4 1.9 %collective-permute-start.3 = (bf16[4,64,640]{2,1,0:T(8,128)(2,1)S(1)}, bf16[4,64,640]{2,1,0:T(8,128)(2,1)S(1)}, u32[]{:S(2)}, u32[]{:S(2)}) collective-permute-start(bf16[4,64,640]{2,1,0:T(8,128)(2,1)S(1)} %get-tuple-element.28), channel_id=1, source_target_pairs={{0,1},{1,2},{2,3},{3,32},{32,33},{33,34},{34,35},{35,64},{64,65},{... | collective-permute-start | bytes 983048 | tf_op jit(solution)/shard_map/ppermute | solution.py:265
  66.3 2.0 %collective-permute-start.4 = (bf16[4,64,640]{2,1,0:T(8,128)(2,1)S(1)}, bf16[4,64,640]{2,1,0:T(8,128)(2,1)S(1)}, u32[]{:S(2)}, u32[]{:S(2)}) collective-permute-start(bf16[4,64,640]{2,1,0:T(8,128)(2,1)S(1)} %get-tuple-element.29), channel_id=1, source_target_pairs={{0,2},{1,99},{2,32},{3,1},{32,34},{33,3},{34,64},{35,33},{64,66},{... | collective-permute-start | bytes 983048 | tf_op jit(solution)/shard_map/ppermute | solution.py:265
  68.4 8.4 %collective-permute-start.5 = (bf16[4,64,640]{2,1,0:T(8,128)(2,1)S(1)}, bf16[4,64,640]{2,1,0:T(8,128)(2,1)S(1)}, u32[]{:S(2)}, u32[]{:S(2)}) collective-permute-start(bf16[4,64,640]{2,1,0:T(8,128)(2,1)S(1)} %get-tuple-element.30), channel_id=1, source_target_pairs={{0,99},{1,0},{2,1},{3,2},{32,3},{33,32},{34,33},{35,34},{64,35},{6... | collective-permute-start | bytes 983048 | tf_op jit(solution)/shard_map/ppermute | solution.py:265
  76.8 5.4 %select_rows.1 = (bf16[8,3,4,24,640]{4,3,2,1,0:T(8,128)(2,1)}, f32[4,64,384]{2,1,0:T(8,128)S(1)}) custom-call(bf16[4,64,1152]{2,1,0:T(8,128)(2,1)S(1)} %bitcast.21, bf16[640,384]{1,0:T(8,128)(2,1)S(1)} %get-tuple-element.26.columns, bf16[4,64,640]{2,1,0:T(8,128)(2,1)} %slice.4.cot0, bf16[4,64,640]{2,1,0:T(8,128)(2,1)} %collective-permute-done.cot1, ...), custom_call_target="tpu_custom_call" | custom-call | flops 754974720 | bytes 5734400 | tf_op jit(solution)/shard_map/select_rows/pallas_call | solution.py:29
  82.2 3.9 %collective-permute-done.4.got2 = bf16[4,64,640]{2,1,0:T(8,128)(2,1)S(1)} collective-permute-done((bf16[4,64,640]{2,1,0:T(8,128)(2,1)S(1)}, bf16[4,64,640]{2,1,0:T(8,128)(2,1)S(1)}, u32[]{:S(2)}, u32[]{:S(2)}) %collective-permute-start.4) | collective-permute-done | bytes 327712 | tf_op jit(solution)/shard_map/ppermute | solution.py:265
  86.1 2.2 %collective-permute-done.5.got3 = bf16[4,64,640]{2,1,0:T(8,128)(2,1)S(1)} collective-permute-done((bf16[4,64,640]{2,1,0:T(8,128)(2,1)S(1)}, bf16[4,64,640]{2,1,0:T(8,128)(2,1)S(1)}, u32[]{:S(2)}, u32[]{:S(2)}) %collective-permute-start.5) | collective-permute-done | bytes 327712 | tf_op jit(solution)/shard_map/ppermute | solution.py:265
  88.3 5.9 %all-to-all-start.1 = ((bf16[8,3,4,24,640]{4,3,2,1,0:T(8,128)(2,1)}), bf16[8,3,4,24,640]{4,3,2,1,0:T(8,128)(2,1)}, u32[]{:S(2)}, u32[]{:S(2)}) async-start(bf16[8,3,4,24,640]{4,3,2,1,0:T(8,128)(2,1)} %get-tuple-element.40), calls=%async_computation.1 | async-start | bytes 5898240 | tf_op jit(solution)/shard_map/all_to_all | solution.py:332
  94.3 5.9 %collective-permute-start.7 = (bf16[64,1024]{1,0:T(8,128)(2,1)S(1)}, bf16[64,1024]{1,0:T(8,128)(2,1)S(1)}, u32[]{:S(2)}, u32[]{:S(2)}) collective-permute-start(bf16[64,1024]{1,0:T(8,128)(2,1)S(1)} %get-tuple-element.38), channel_id=1, source_target_pairs={{0,32},{4,100},{32,64},{36,4},{64,96},{68,36},{96,0},{100,68},{1,3... | collective-permute-start | bytes 393224 | tf_op jit(solution)/shard_map/ppermute | solution.py:250
  100.2 3.3 %collective-permute-start.6 = (bf16[64,1024]{1,0:T(8,128)(2,1)S(1)}, bf16[64,1024]{1,0:T(8,128)(2,1)S(1)}, u32[]{:S(2)}, u32[]{:S(2)}) collective-permute-start(bf16[64,1024]{1,0:T(8,128)(2,1)S(1)} %get-tuple-element.36), channel_id=1, source_target_pairs={{0,96},{4,36},{32,0},{36,68},{64,32},{68,100},{96,64},{100,4},{1,9... | collective-permute-start | bytes 393224 | tf_op jit(solution)/shard_map/ppermute | solution.py:250
  105.3 7.2 %collective-permute-start.8 = (bf16[64,1024]{1,0:T(8,128)(2,1)S(1)}, bf16[64,1024]{1,0:T(8,128)(2,1)S(1)}, u32[]{:S(2)}, u32[]{:S(2)}) collective-permute-start(bf16[64,1024]{1,0:T(8,128)(2,1)S(1)} %z_relay.1), channel_id=1, source_target_pairs={{0,32},{4,100},{32,64},{36,4},{64,96},{68,36},{96,0},{100,68},{1,3... | collective-permute-start | bytes 393224 | tf_op jit(solution)/shard_map/ppermute | solution.py:250
  112.5 3.0 %collective-permute-done.6.got1 = bf16[64,1024]{1,0:T(8,128)(2,1)S(1)} collective-permute-done((bf16[64,1024]{1,0:T(8,128)(2,1)S(1)}, bf16[64,1024]{1,0:T(8,128)(2,1)S(1)}, u32[]{:S(2)}, u32[]{:S(2)}) %collective-permute-start.6) | collective-permute-done | bytes 131104 | tf_op jit(solution)/shard_map/ppermute | solution.py:250
  115.5 3.8 %collective-permute-done.8.got2 = bf16[64,1024]{1,0:T(8,128)(2,1)S(1)} collective-permute-done((bf16[64,1024]{1,0:T(8,128)(2,1)S(1)}, bf16[64,1024]{1,0:T(8,128)(2,1)S(1)}, u32[]{:S(2)}, u32[]{:S(2)}) %collective-permute-start.8) | collective-permute-done | bytes 131104 | tf_op jit(solution)/shard_map/ppermute | solution.py:250
  120.0 3.1 %collective-permute-start.9 = (bf16[64,640]{1,0:T(8,128)(2,1)S(1)}, bf16[64,640]{1,0:T(8,128)(2,1)S(1)}, u32[]{:S(2)}, u32[]{:S(2)}) collective-permute-start(bf16[64,640]{1,0:T(8,128)(2,1)S(1)} %get-tuple-element.39), channel_id=1, source_target_pairs={{0,128},{128,256},{256,384},{384,0},{1,129},{129,257},{257,385},{3... | collective-permute-start | bytes 245768 | tf_op jit(solution)/shard_map/ppermute | solution.py:254
  123.1 3.7 %collective-permute-done.9 = bf16[64,640]{1,0:T(8,128)(2,1)S(1)} collective-permute-done((bf16[64,640]{1,0:T(8,128)(2,1)S(1)}, bf16[64,640]{1,0:T(8,128)(2,1)S(1)}, u32[]{:S(2)}, u32[]{:S(2)}) %collective-permute-start.9) | collective-permute-done | bytes 81952 | tf_op jit(solution)/shard_map/ppermute | solution.py:254
  126.8 2.9 %all-to-all-done.1.rows = bf16[8,3,4,24,640]{4,3,2,1,0:T(8,128)(2,1)} async-done(((bf16[8,3,4,24,640]{4,3,2,1,0:T(8,128)(2,1)}), bf16[8,3,4,24,640]{4,3,2,1,0:T(8,128)(2,1)}, u32[]{:S(2)}, u32[]{:S(2)}) %all-to-all-start.1) | async-done | bytes 2949152 | tf_op jit(solution)/shard_map/all_to_all | solution.py:332
  129.7 5.3 %hidden_back.1 = bf16[3,6,32,256]{3,2,1,0:T(8,128)(2,1)} custom-call(bf16[8,3,4,24,640]{4,3,2,1,0:T(8,128)(2,1)} %all-to-all-done.1.rows, bf16[3,256,2560]{2,1,0:T(8,128)(2,1)} %bitcast.23), custom_call_target="tpu_custom_call" | custom-call | flops 754974720 | bytes 7000000 | tf_op jit(solution)/shard_map/hidden_back/pallas_call | solution.py:349
  (18 shorter events, 6.0 us)
Async XLA Ops:
  6.4 51.2 %all-to-all-start = ((bf16[8,14,24,640]{3,2,1,0:T(8,128)(2,1)}), bf16[8,14,24,640]{3,2,1,0:T(8,128)(2,1)S(1)}, u32[]{:S(2)}, u32[]{:S(2)}) async-start(bf16[8,14,24,640]{3,2,1,0:T(8,128)(2,1)} %get-tuple-element.24), calls=%async_computation | async-start | bytes 6881280 | tf_op jit(solution)/shard_map/all_to_all | solution.py:306
  45.3 7.0 %copy-start = (bf16[256,1152]{1,0:T(8,128)(2,1)}, bf16[256,1152]{1,0:T(8,128)(2,1)S(1)}, u32[]{:S(2)}) copy-start(bf16[256,1152]{1,0:T(8,128)(2,1)S(1)} %all-gather) | copy-start | bytes 1769476
  46.2 22.2 %collective-permute-start.2 = (bf16[4,64,640]{2,1,0:T(8,128)(2,1)}, bf16[4,64,640]{2,1,0:T(8,128)(2,1)}, u32[]{:S(2)}, u32[]{:S(2)}) collective-permute-start(bf16[4,64,640]{2,1,0:T(8,128)(2,1)} %slice.4.cot0), channel_id=1, source_target_pairs={{0,1},{1,2},{2,3},{3,32},{32,33},{33,34},{34,35},{35,64},{64,65},{... | collective-permute-start | bytes 983048 | tf_op jit(solution)/shard_map/ppermute | solution.py:265
  48.1 28.7 %collective-permute-start.1 = (bf16[4,64,640]{2,1,0:T(8,128)(2,1)}, bf16[4,64,640]{2,1,0:T(8,128)(2,1)}, u32[]{:S(2)}, u32[]{:S(2)}) collective-permute-start(bf16[4,64,640]{2,1,0:T(8,128)(2,1)} %slice.4.cot0), channel_id=1, source_target_pairs={{0,2},{1,99},{2,32},{3,1},{32,34},{33,3},{34,64},{35,33},{64,66},{... | collective-permute-start | bytes 983048 | tf_op jit(solution)/shard_map/ppermute | solution.py:265
  52.3 24.5 %collective-permute-start = (bf16[4,64,640]{2,1,0:T(8,128)(2,1)}, bf16[4,64,640]{2,1,0:T(8,128)(2,1)}, u32[]{:S(2)}, u32[]{:S(2)}) collective-permute-start(bf16[4,64,640]{2,1,0:T(8,128)(2,1)} %slice.4.cot0), channel_id=1, source_target_pairs={{0,99},{1,0},{2,1},{3,2},{32,3},{33,32},{34,33},{35,34},{64,35},{6... | collective-permute-start | bytes 983048 | tf_op jit(solution)/shard_map/ppermute | solution.py:265
  57.6 1.1 copy-start.1
  63.5 0.9 copy-start.2
  64.4 17.8 %collective-permute-start.3 = (bf16[4,64,640]{2,1,0:T(8,128)(2,1)S(1)}, bf16[4,64,640]{2,1,0:T(8,128)(2,1)S(1)}, u32[]{:S(2)}, u32[]{:S(2)}) collective-permute-start(bf16[4,64,640]{2,1,0:T(8,128)(2,1)S(1)} %get-tuple-element.28), channel_id=1, source_target_pairs={{0,1},{1,2},{2,3},{3,32},{32,33},{33,34},{34,35},{35,64},{64,65},{... | collective-permute-start | bytes 983048 | tf_op jit(solution)/shard_map/ppermute | solution.py:265
  66.3 19.7 %collective-permute-start.4 = (bf16[4,64,640]{2,1,0:T(8,128)(2,1)S(1)}, bf16[4,64,640]{2,1,0:T(8,128)(2,1)S(1)}, u32[]{:S(2)}, u32[]{:S(2)}) collective-permute-start(bf16[4,64,640]{2,1,0:T(8,128)(2,1)S(1)} %get-tuple-element.29), channel_id=1, source_target_pairs={{0,2},{1,99},{2,32},{3,1},{32,34},{33,3},{34,64},{35,33},{64,66},{... | collective-permute-start | bytes 983048 | tf_op jit(solution)/shard_map/ppermute | solution.py:265
  68.4 19.9 %collective-permute-start.5 = (bf16[4,64,640]{2,1,0:T(8,128)(2,1)S(1)}, bf16[4,64,640]{2,1,0:T(8,128)(2,1)S(1)}, u32[]{:S(2)}, u32[]{:S(2)}) collective-permute-start(bf16[4,64,640]{2,1,0:T(8,128)(2,1)S(1)} %get-tuple-element.30), channel_id=1, source_target_pairs={{0,99},{1,0},{2,1},{3,2},{32,3},{33,32},{34,33},{35,34},{64,35},{6... | collective-permute-start | bytes 983048 | tf_op jit(solution)/shard_map/ppermute | solution.py:265
  82.2 12.0 %copy-start.3 = (f32[4,64,640]{2,1,0:T(8,128)S(1)}, f32[4,64,640]{2,1,0:T(8,128)}, u32[]{:S(2)}) copy-start(f32[4,64,640]{2,1,0:T(8,128)} %copy-done.2) | copy-start | bytes 1966084
  88.3 41.4 %all-to-all-start.1 = ((bf16[8,3,4,24,640]{4,3,2,1,0:T(8,128)(2,1)}), bf16[8,3,4,24,640]{4,3,2,1,0:T(8,128)(2,1)}, u32[]{:S(2)}, u32[]{:S(2)}) async-start(bf16[8,3,4,24,640]{4,3,2,1,0:T(8,128)(2,1)} %get-tuple-element.40), calls=%async_computation.1 | async-start | bytes 5898240 | tf_op jit(solution)/shard_map/all_to_all | solution.py:332
  94.3 11.0 %collective-permute-start.7 = (bf16[64,1024]{1,0:T(8,128)(2,1)S(1)}, bf16[64,1024]{1,0:T(8,128)(2,1)S(1)}, u32[]{:S(2)}, u32[]{:S(2)}) collective-permute-start(bf16[64,1024]{1,0:T(8,128)(2,1)S(1)} %get-tuple-element.38), channel_id=1, source_target_pairs={{0,32},{4,100},{32,64},{36,4},{64,96},{68,36},{96,0},{100,68},{1,3... | collective-permute-start | bytes 393224 | tf_op jit(solution)/shard_map/ppermute | solution.py:250
  100.2 15.3 %collective-permute-start.6 = (bf16[64,1024]{1,0:T(8,128)(2,1)S(1)}, bf16[64,1024]{1,0:T(8,128)(2,1)S(1)}, u32[]{:S(2)}, u32[]{:S(2)}) collective-permute-start(bf16[64,1024]{1,0:T(8,128)(2,1)S(1)} %get-tuple-element.36), channel_id=1, source_target_pairs={{0,96},{4,36},{32,0},{36,68},{64,32},{68,100},{96,64},{100,4},{1,9... | collective-permute-start | bytes 393224 | tf_op jit(solution)/shard_map/ppermute | solution.py:250
  105.3 14.1 %collective-permute-start.8 = (bf16[64,1024]{1,0:T(8,128)(2,1)S(1)}, bf16[64,1024]{1,0:T(8,128)(2,1)S(1)}, u32[]{:S(2)}, u32[]{:S(2)}) collective-permute-start(bf16[64,1024]{1,0:T(8,128)(2,1)S(1)} %z_relay.1), channel_id=1, source_target_pairs={{0,32},{4,100},{32,64},{36,4},{64,96},{68,36},{96,0},{100,68},{1,3... | collective-permute-start | bytes 393224 | tf_op jit(solution)/shard_map/ppermute | solution.py:250
  120.0 6.8 %collective-permute-start.9 = (bf16[64,640]{1,0:T(8,128)(2,1)S(1)}, bf16[64,640]{1,0:T(8,128)(2,1)S(1)}, u32[]{:S(2)}, u32[]{:S(2)}) collective-permute-start(bf16[64,640]{1,0:T(8,128)(2,1)S(1)} %get-tuple-element.39), channel_id=1, source_target_pairs={{0,128},{128,256},{256,384},{384,0},{1,129},{129,257},{257,385},{3... | collective-permute-start | bytes 245768 | tf_op jit(solution)/shard_map/ppermute | solution.py:254

commit v4 on v3

--- a/solution.py
+++ b/solution.py
@@ -328,7 +328,7 @@
         name="select_rows",
         vmem=14,
     )
-    outgoing, *got = lax.optimization_barrier((outgoing, *got))
+    outgoing, got[0], got[1] = lax.optimization_barrier((outgoing, got[0], got[1]))
     received = lax.all_to_all(outgoing, ("y", "core"), 0, 0, tiled=True)
 
     own, held, far, near = call(

time: 136 us -> 146 us (1.074)
  the two profiles are of different devices: /device:TPU:1 before, /device:TPU:8 now
where the time goes in v4:
time: 146 us; the launch traced here: 145 us
  starting transfers between devices  54.5 us (37%)
  waiting for transfers between devices  33 us (23%)
  blocking collectives  31.7 us (22%)
  Pallas kernels  22.1 us (15%)
  local copies, waits for them, and re-layouts  3.36 us (2%)
    all_gather x1, blocking collectives, on_device(): whole = lax.all_gather(packed, 'zhi', axis=0, tiled=False)  31.7 us
    ppermute x6, waiting for transfers between devices, over_z(): return lax.ppermute(value, ('zhi', 'tensor'), z_pairs(step))  18.6 us
    ppermute x3, starting transfers between devices, ahead(): return lax.ppermute(value, ('zhi', 'core'), pairs)  18 us
    ppermute x6, starting transfers between devices, over_z(): return lax.ppermute(value, ('zhi', 'tensor'), z_pairs(step))  17.8 us
    pallas_call x5, Pallas kernels, call(): pl.pallas_call(body, out_shape=out_shape, in_specs=[VM] * len(args), out_...  11 us
    ppermute x3, waiting for transfers between devices, ahead(): return lax.ppermute(value, ('zhi', 'core'), pairs)  10.2 us
    all_to_all x1, starting transfers between devices, on_device(): arrived = lax.all_to_all(parts, ('y', 'core'), 0, 0, tiled=True)  9.4 us
    all_to_all x1, starting transfers between devices, on_device(): received = lax.all_to_all(outgoing, ('y', 'core'), 0, 0, tiled=True)  5.91 us
  transfers between devices with their start and end apart: 12, of which 7 were waited for; matrix products, arithmetic and copies ran while one was open for 1% of the time, Pallas kernels for 8%

profile of v4, /device:TPU:8, one launch (start us, length us, event | category | flops | bytes accessed | tf_op | source)
XLA Modules:
  0.0 145.4 jit_solution(4854709474445025617)
XLA Ops:
  0.6 5.8 %expert_rows.1 = (bf16[8,14,24,640]{3,2,1,0:T(8,128)(2,1)}, bf16[64,1152]{1,0:T(8,128)(2,1)}) custom-call(bf16[3,6,32,256]{3,2,1,0:T(8,128)(2,1)} %bitcast.25, bf16[3,256,2560]{2,1,0:T(8,128)(2,1)} %bitcast.22, bf16[80,384]{1,0:T(8,128)(2,1)} %bitcast.28, s32[6,1,64]{2,1,0:T(1,128)} %bitcast.30, f32[6,1,64]{2,1,0:T(1,128)} %bitcast.31, ...), custom_call_target="tpu_custom_call" | custom-call | flops 754974720 | bytes 8000000 | tf_op jit(solution)/shard_map/expert_rows/pallas_call | solution.py:287
  6.4 9.4 %all-to-all-start = ((bf16[8,14,24,640]{3,2,1,0:T(8,128)(2,1)}), bf16[8,14,24,640]{3,2,1,0:T(8,128)(2,1)S(1)}, u32[]{:S(2)}, u32[]{:S(2)}) async-start(bf16[8,14,24,640]{3,2,1,0:T(8,128)(2,1)} %get-tuple-element.23), calls=%async_computation | async-start | bytes 6881280 | tf_op jit(solution)/shard_map/all_to_all | solution.py:306
  15.8 31.7 %all-gather = bf16[256,1152]{1,0:T(8,128)(2,1)S(1)} all-gather(bf16[64,1152]{1,0:T(8,128)(2,1)} %get-tuple-element.22), channel_id=2, replica_groups=mesh['phase'=4,'zhi'=4,'y'=4,'core'=2,'tensor'=4] {'zhi'}, dimensions={0}, use_global_device_ids=true | all-gather | bytes 737280 | tf_op jit(solution)/shard_map/all_gather | solution.py:308
  48.3 2.5 %collective-permute-start.2 = (bf16[4,64,640]{2,1,0:T(8,128)(2,1)}, bf16[4,64,640]{2,1,0:T(8,128)(2,1)}, u32[]{:S(2)}, u32[]{:S(2)}) collective-permute-start(bf16[4,64,640]{2,1,0:T(8,128)(2,1)} %slice.4.cot0), channel_id=1, source_target_pairs={{0,1},{1,2},{2,3},{3,32},{32,33},{33,34},{34,35},{35,64},{64,65},{... | collective-permute-start | bytes 983048 | tf_op jit(solution)/shard_map/ppermute | solution.py:265
  50.9 3.8 %collective-permute-start.1 = (bf16[4,64,640]{2,1,0:T(8,128)(2,1)}, bf16[4,64,640]{2,1,0:T(8,128)(2,1)}, u32[]{:S(2)}, u32[]{:S(2)}) collective-permute-start(bf16[4,64,640]{2,1,0:T(8,128)(2,1)} %slice.4.cot0), channel_id=1, source_target_pairs={{0,2},{1,99},{2,32},{3,1},{32,34},{33,3},{34,64},{35,33},{64,66},{... | collective-permute-start | bytes 983048 | tf_op jit(solution)/shard_map/ppermute | solution.py:265
  54.7 3.4 %collective-permute-start = (bf16[4,64,640]{2,1,0:T(8,128)(2,1)}, bf16[4,64,640]{2,1,0:T(8,128)(2,1)}, u32[]{:S(2)}, u32[]{:S(2)}) collective-permute-start(bf16[4,64,640]{2,1,0:T(8,128)(2,1)} %slice.4.cot0), channel_id=1, source_target_pairs={{0,99},{1,0},{2,1},{3,2},{32,3},{33,32},{34,33},{35,34},{64,35},{6... | collective-permute-start | bytes 983048 | tf_op jit(solution)/shard_map/ppermute | solution.py:265
  58.1 1.1 copy-done.1
  59.2 4.8 %combine.1 = (f32[4,64,640]{2,1,0:T(8,128)S(1)}, bf16[4,64,640]{2,1,0:T(8,128)(2,1)S(1)}, bf16[4,64,640]{2,1,0:T(8,128)(2,1)S(1)}, bf16[4,64,640]{2,1,0:T(8,128)(2,1)S(1)}, bf16[640,384]{1,0:T(8,128)(2,1)S(1)}) custom-call(bf16[4,64,1152]{2,1,0:T(8,128)(2,1)S(1)} %bitcast.20, bf16[8,14,24,640]{3,2,1,0:T(8,128)(2,1)S(1)} %all-to-all-done.rows), custom_call_target="tpu_custom_call" | custom-call | flops 2264924160 | bytes 6160384 | tf_op jit(solution)/shard_map/combine/pallas_call | solution.py:29
  64.8 2.6 %collective-permute-start.3 = (bf16[4,64,640]{2,1,0:T(8,128)(2,1)S(1)}, bf16[4,64,640]{2,1,0:T(8,128)(2,1)S(1)}, u32[]{:S(2)}, u32[]{:S(2)}) collective-permute-start(bf16[4,64,640]{2,1,0:T(8,128)(2,1)S(1)} %get-tuple-element.27), channel_id=1, source_target_pairs={{0,1},{1,2},{2,3},{3,32},{32,33},{33,34},{34,35},{35,64},{64,65},{... | collective-permute-start | bytes 983048 | tf_op jit(solution)/shard_map/ppermute | solution.py:265
  67.4 3.6 %collective-permute-start.4 = (bf16[4,64,640]{2,1,0:T(8,128)(2,1)S(1)}, bf16[4,64,640]{2,1,0:T(8,128)(2,1)S(1)}, u32[]{:S(2)}, u32[]{:S(2)}) collective-permute-start(bf16[4,64,640]{2,1,0:T(8,128)(2,1)S(1)} %get-tuple-element.28), channel_id=1, source_target_pairs={{0,2},{1,99},{2,32},{3,1},{32,34},{33,3},{34,64},{35,33},{64,66},{... | collective-permute-start | bytes 983048 | tf_op jit(solution)/shard_map/ppermute | solution.py:265
  71.1 5.4 %select_rows.1 = (bf16[8,3,4,24,640]{4,3,2,1,0:T(8,128)(2,1)}, f32[4,64,384]{2,1,0:T(8,128)S(1)}) custom-call(bf16[4,64,1152]{2,1,0:T(8,128)(2,1)S(1)} %bitcast.21, bf16[640,384]{1,0:T(8,128)(2,1)S(1)} %get-tuple-element.25.columns, bf16[4,64,640]{2,1,0:T(8,128)(2,1)} %slice.4.cot0, bf16[4,64,640]{2,1,0:T(8,128)(2,1)} %collective-permute-done.cot1, ...), custom_call_target="tpu_custom_call" | custom-call | flops 754974720 | bytes 5734400 | tf_op jit(solution)/shard_map/select_rows/pallas_call | solution.py:29
  77.3 8.0 %collective-permute-done.4.got2 = bf16[4,64,640]{2,1,0:T(8,128)(2,1)S(1)} collective-permute-done((bf16[4,64,640]{2,1,0:T(8,128)(2,1)S(1)}, bf16[4,64,640]{2,1,0:T(8,128)(2,1)S(1)}, u32[]{:S(2)}, u32[]{:S(2)}) %collective-permute-start.4) | collective-permute-done | bytes 327712 | tf_op jit(solution)/shard_map/ppermute | solution.py:265
  85.3 5.9 %all-to-all-start.1 = ((bf16[8,3,4,24,640]{4,3,2,1,0:T(8,128)(2,1)}), bf16[8,3,4,24,640]{4,3,2,1,0:T(8,128)(2,1)}, u32[]{:S(2)}, u32[]{:S(2)}) async-start(bf16[8,3,4,24,640]{4,3,2,1,0:T(8,128)(2,1)} %get-tuple-element.38), calls=%async_computation.1 | async-start | bytes 5898240 | tf_op jit(solution)/shard_map/all_to_all | solution.py:332
  91.3 1.9 %collective-permute-start.5 = (bf16[4,64,640]{2,1,0:T(8,128)(2,1)S(1)}, bf16[4,64,640]{2,1,0:T(8,128)(2,1)S(1)}, u32[]{:S(2)}, u32[]{:S(2)}) collective-permute-start(bf16[4,64,640]{2,1,0:T(8,128)(2,1)S(1)} %copy-done.5), channel_id=1, source_target_pairs={{0,99},{1,0},{2,1},{3,2},{32,3},{33,32},{34,33},{35,34},{64,35},{6... | collective-permute-start | bytes 983048 | tf_op jit(solution)/shard_map/ppermute | solution.py:265
  93.2 9.7 %collective-permute-done.5.got3 = bf16[4,64,640]{2,1,0:T(8,128)(2,1)S(1)} collective-permute-done((bf16[4,64,640]{2,1,0:T(8,128)(2,1)S(1)}, bf16[4,64,640]{2,1,0:T(8,128)(2,1)S(1)}, u32[]{:S(2)}, u32[]{:S(2)}) %collective-permute-start.5) | collective-permute-done | bytes 327712 | tf_op jit(solution)/shard_map/ppermute | solution.py:265
  103.0 1.9 %collective-permute-start.7 = (bf16[64,1024]{1,0:T(8,128)(2,1)S(1)}, bf16[64,1024]{1,0:T(8,128)(2,1)S(1)}, u32[]{:S(2)}, u32[]{:S(2)}) collective-permute-start(bf16[64,1024]{1,0:T(8,128)(2,1)S(1)} %get-tuple-element.36), channel_id=1, source_target_pairs={{0,32},{4,100},{32,64},{36,4},{64,96},{68,36},{96,0},{100,68},{1,3... | collective-permute-start | bytes 393224 | tf_op jit(solution)/shard_map/ppermute | solution.py:250
  105.0 7.8 %collective-permute-start.6 = (bf16[64,1024]{1,0:T(8,128)(2,1)S(1)}, bf16[64,1024]{1,0:T(8,128)(2,1)S(1)}, u32[]{:S(2)}, u32[]{:S(2)}) collective-permute-start(bf16[64,1024]{1,0:T(8,128)(2,1)S(1)} %get-tuple-element.34), channel_id=1, source_target_pairs={{0,96},{4,36},{32,0},{36,68},{64,32},{68,100},{96,64},{100,4},{1,9... | collective-permute-start | bytes 393224 | tf_op jit(solution)/shard_map/ppermute | solution.py:250
  112.8 3.3 %collective-permute-done.7.passing = bf16[64,1024]{1,0:T(8,128)(2,1)S(1)} collective-permute-done((bf16[64,1024]{1,0:T(8,128)(2,1)S(1)}, bf16[64,1024]{1,0:T(8,128)(2,1)S(1)}, u32[]{:S(2)}, u32[]{:S(2)}) %collective-permute-start.7) | collective-permute-done | bytes 131104 | tf_op jit(solution)/shard_map/ppermute | solution.py:250
  116.2 8.2 %collective-permute-start.8 = (bf16[64,1024]{1,0:T(8,128)(2,1)S(1)}, bf16[64,1024]{1,0:T(8,128)(2,1)S(1)}, u32[]{:S(2)}, u32[]{:S(2)}) collective-permute-start(bf16[64,1024]{1,0:T(8,128)(2,1)S(1)} %z_relay.1), channel_id=1, source_target_pairs={{0,32},{4,100},{32,64},{36,4},{64,96},{68,36},{96,0},{100,68},{1,3... | collective-permute-start | bytes 393224 | tf_op jit(solution)/shard_map/ppermute | solution.py:250
  124.4 0.9 collective-permute-done.6.got1
  125.4 5.9 %collective-permute-done.8.got2 = bf16[64,1024]{1,0:T(8,128)(2,1)S(1)} collective-permute-done((bf16[64,1024]{1,0:T(8,128)(2,1)S(1)}, bf16[64,1024]{1,0:T(8,128)(2,1)S(1)}, u32[]{:S(2)}, u32[]{:S(2)}) %collective-permute-start.8) | collective-permute-done | bytes 131104 | tf_op jit(solution)/shard_map/ppermute | solution.py:250
  131.9 3.4 %collective-permute-start.9 = (bf16[64,640]{1,0:T(8,128)(2,1)S(1)}, bf16[64,640]{1,0:T(8,128)(2,1)S(1)}, u32[]{:S(2)}, u32[]{:S(2)}) collective-permute-start(bf16[64,640]{1,0:T(8,128)(2,1)S(1)} %get-tuple-element.37), channel_id=1, source_target_pairs={{0,128},{128,256},{256,384},{384,0},{1,129},{129,257},{257,385},{3... | collective-permute-start | bytes 245768 | tf_op jit(solution)/shard_map/ppermute | solution.py:254
  135.3 4.1 %collective-permute-done.9 = bf16[64,640]{1,0:T(8,128)(2,1)S(1)} collective-permute-done((bf16[64,640]{1,0:T(8,128)(2,1)S(1)}, bf16[64,640]{1,0:T(8,128)(2,1)S(1)}, u32[]{:S(2)}, u32[]{:S(2)}) %collective-permute-start.9) | collective-permute-done | bytes 81952 | tf_op jit(solution)/shard_map/ppermute | solution.py:254
  139.4 5.3 %hidden_back.1 = bf16[3,6,32,256]{3,2,1,0:T(8,128)(2,1)} custom-call(bf16[8,3,4,24,640]{4,3,2,1,0:T(8,128)(2,1)} %all-to-all-done.1.rows, bf16[3,256,2560]{2,1,0:T(8,128)(2,1)} %bitcast.23), custom_call_target="tpu_custom_call" | custom-call | flops 754974720 | bytes 7000000 | tf_op jit(solution)/shard_map/hidden_back/pallas_call | solution.py:349
  (22 shorter events, 4.0 us)
Async XLA Ops:
  6.4 51.7 %all-to-all-start = ((bf16[8,14,24,640]{3,2,1,0:T(8,128)(2,1)}), bf16[8,14,24,640]{3,2,1,0:T(8,128)(2,1)S(1)}, u32[]{:S(2)}, u32[]{:S(2)}) async-start(bf16[8,14,24,640]{3,2,1,0:T(8,128)(2,1)} %get-tuple-element.23), calls=%async_computation | async-start | bytes 6881280 | tf_op jit(solution)/shard_map/all_to_all | solution.py:306
  47.5 7.2 %copy-start = (bf16[256,1152]{1,0:T(8,128)(2,1)}, bf16[256,1152]{1,0:T(8,128)(2,1)S(1)}, u32[]{:S(2)}) copy-start(bf16[256,1152]{1,0:T(8,128)(2,1)S(1)} %all-gather) | copy-start | bytes 1769476
  48.3 22.7 %collective-permute-start.2 = (bf16[4,64,640]{2,1,0:T(8,128)(2,1)}, bf16[4,64,640]{2,1,0:T(8,128)(2,1)}, u32[]{:S(2)}, u32[]{:S(2)}) collective-permute-start(bf16[4,64,640]{2,1,0:T(8,128)(2,1)} %slice.4.cot0), channel_id=1, source_target_pairs={{0,1},{1,2},{2,3},{3,32},{32,33},{33,34},{34,35},{35,64},{64,65},{... | collective-permute-start | bytes 983048 | tf_op jit(solution)/shard_map/ppermute | solution.py:265
  50.9 20.2 %collective-permute-start.1 = (bf16[4,64,640]{2,1,0:T(8,128)(2,1)}, bf16[4,64,640]{2,1,0:T(8,128)(2,1)}, u32[]{:S(2)}, u32[]{:S(2)}) collective-permute-start(bf16[4,64,640]{2,1,0:T(8,128)(2,1)} %slice.4.cot0), channel_id=1, source_target_pairs={{0,2},{1,99},{2,32},{3,1},{32,34},{33,3},{34,64},{35,33},{64,66},{... | collective-permute-start | bytes 983048 | tf_op jit(solution)/shard_map/ppermute | solution.py:265
  54.7 16.4 %collective-permute-start = (bf16[4,64,640]{2,1,0:T(8,128)(2,1)}, bf16[4,64,640]{2,1,0:T(8,128)(2,1)}, u32[]{:S(2)}, u32[]{:S(2)}) collective-permute-start(bf16[4,64,640]{2,1,0:T(8,128)(2,1)} %slice.4.cot0), channel_id=1, source_target_pairs={{0,99},{1,0},{2,1},{3,2},{32,3},{33,32},{34,33},{35,34},{64,35},{6... | collective-permute-start | bytes 983048 | tf_op jit(solution)/shard_map/ppermute | solution.py:265
  58.1 1.1 copy-start.1
  64.0 0.8 copy-start.2
  64.8 20.5 %copy-start.4 = (bf16[4,64,640]{2,1,0:T(8,128)(2,1)}, bf16[4,64,640]{2,1,0:T(8,128)(2,1)S(1)}, u32[]{:S(2)}) copy-start(bf16[4,64,640]{2,1,0:T(8,128)(2,1)S(1)} %get-tuple-element.31) | copy-start | bytes 983044
  64.8 12.5 %collective-permute-start.3 = (bf16[4,64,640]{2,1,0:T(8,128)(2,1)S(1)}, bf16[4,64,640]{2,1,0:T(8,128)(2,1)S(1)}, u32[]{:S(2)}, u32[]{:S(2)}) collective-permute-start(bf16[4,64,640]{2,1,0:T(8,128)(2,1)S(1)} %get-tuple-element.27), channel_id=1, source_target_pairs={{0,1},{1,2},{2,3},{3,32},{32,33},{33,34},{34,35},{35,64},{64,65},{... | collective-permute-start | bytes 983048 | tf_op jit(solution)/shard_map/ppermute | solution.py:265
  67.4 17.9 %collective-permute-start.4 = (bf16[4,64,640]{2,1,0:T(8,128)(2,1)S(1)}, bf16[4,64,640]{2,1,0:T(8,128)(2,1)S(1)}, u32[]{:S(2)}, u32[]{:S(2)}) collective-permute-start(bf16[4,64,640]{2,1,0:T(8,128)(2,1)S(1)} %get-tuple-element.28), channel_id=1, source_target_pairs={{0,2},{1,99},{2,32},{3,1},{32,34},{33,3},{34,64},{35,33},{64,66},{... | collective-permute-start | bytes 983048 | tf_op jit(solution)/shard_map/ppermute | solution.py:265
  76.4 26.5 %copy-start.3 = (f32[4,64,640]{2,1,0:T(8,128)S(1)}, f32[4,64,640]{2,1,0:T(8,128)}, u32[]{:S(2)}) copy-start(f32[4,64,640]{2,1,0:T(8,128)} %copy-done.2) | copy-start | bytes 1966084
  85.3 5.9 %copy-start.5 = (bf16[4,64,640]{2,1,0:T(8,128)(2,1)S(1)}, bf16[4,64,640]{2,1,0:T(8,128)(2,1)}, u32[]{:S(2)}) copy-start(bf16[4,64,640]{2,1,0:T(8,128)(2,1)} %copy-done.4) | copy-start | bytes 983044
  85.3 54.1 %all-to-all-start.1 = ((bf16[8,3,4,24,640]{4,3,2,1,0:T(8,128)(2,1)}), bf16[8,3,4,24,640]{4,3,2,1,0:T(8,128)(2,1)}, u32[]{:S(2)}, u32[]{:S(2)}) async-start(bf16[8,3,4,24,640]{4,3,2,1,0:T(8,128)(2,1)} %get-tuple-element.38), calls=%async_computation.1 | async-start | bytes 5898240 | tf_op jit(solution)/shard_map/all_to_all | solution.py:332
  91.3 11.6 %collective-permute-start.5 = (bf16[4,64,640]{2,1,0:T(8,128)(2,1)S(1)}, bf16[4,64,640]{2,1,0:T(8,128)(2,1)S(1)}, u32[]{:S(2)}, u32[]{:S(2)}) collective-permute-start(bf16[4,64,640]{2,1,0:T(8,128)(2,1)S(1)} %copy-done.5), channel_id=1, source_target_pairs={{0,99},{1,0},{2,1},{3,2},{32,3},{33,32},{34,33},{35,34},{64,35},{6... | collective-permute-start | bytes 983048 | tf_op jit(solution)/shard_map/ppermute | solution.py:265
  103.0 13.1 %collective-permute-start.7 = (bf16[64,1024]{1,0:T(8,128)(2,1)S(1)}, bf16[64,1024]{1,0:T(8,128)(2,1)S(1)}, u32[]{:S(2)}, u32[]{:S(2)}) collective-permute-start(bf16[64,1024]{1,0:T(8,128)(2,1)S(1)} %get-tuple-element.36), channel_id=1, source_target_pairs={{0,32},{4,100},{32,64},{36,4},{64,96},{68,36},{96,0},{100,68},{1,3... | collective-permute-start | bytes 393224 | tf_op jit(solution)/shard_map/ppermute | solution.py:250
  105.0 20.4 %collective-permute-start.6 = (bf16[64,1024]{1,0:T(8,128)(2,1)S(1)}, bf16[64,1024]{1,0:T(8,128)(2,1)S(1)}, u32[]{:S(2)}, u32[]{:S(2)}) collective-permute-start(bf16[64,1024]{1,0:T(8,128)(2,1)S(1)} %get-tuple-element.34), channel_id=1, source_target_pairs={{0,96},{4,36},{32,0},{36,68},{64,32},{68,100},{96,64},{100,4},{1,9... | collective-permute-start | bytes 393224 | tf_op jit(solution)/shard_map/ppermute | solution.py:250
  116.2 15.1 %collective-permute-start.8 = (bf16[64,1024]{1,0:T(8,128)(2,1)S(1)}, bf16[64,1024]{1,0:T(8,128)(2,1)S(1)}, u32[]{:S(2)}, u32[]{:S(2)}) collective-permute-start(bf16[64,1024]{1,0:T(8,128)(2,1)S(1)} %z_relay.1), channel_id=1, source_target_pairs={{0,32},{4,100},{32,64},{36,4},{64,96},{68,36},{96,0},{100,68},{1,3... | collective-permute-start | bytes 393224 | tf_op jit(solution)/shard_map/ppermute | solution.py:250
  131.9 7.5 %collective-permute-start.9 = (bf16[64,640]{1,0:T(8,128)(2,1)S(1)}, bf16[64,640]{1,0:T(8,128)(2,1)S(1)}, u32[]{:S(2)}, u32[]{:S(2)}) collective-permute-start(bf16[64,640]{1,0:T(8,128)(2,1)S(1)} %get-tuple-element.37), channel_id=1, source_target_pairs={{0,128},{128,256},{256,384},{384,0},{1,129},{129,257},{257,385},{3... | collective-permute-start | bytes 245768 | tf_op jit(solution)/shard_map/ppermute | solution.py:254
